TPU v7x, 512 devices: a whole 4x8x8 slice. The times are simulated.
512 devices in a mesh: section: 8 (over y), expert: 64 (over x, z, core).
Axes of the slice: x: 4, y: 8, z: 8, core: 2. Of those that a mesh axis runs over, the one named last changes fastest.
Arguments:
- section_input: bfloat16 [8, 6144, 2048], P('section', 'expert'), may hold values from -6 to 6
- saved_input: bfloat16 [8, 6144, 2048], P('section', 'expert'), may hold values from -6 to 6
- grad_input: bfloat16 [8, 6144, 2048], P('section', 'expert'), may hold values from -6 to 6
- expert_ids: int32 [8, 2, 6144, 2], P('section', None, 'expert'), may hold values from 0 to 15, all different within a row; in each aligned block of 96 rows (0 to 95, 96 to 191, ..., all dimensions but the last counted through in order) at most 16 rows name the same one
- keep_mask: int32 [8, 2, 6144, 2], P('section', None, 'expert'), may hold values 0 or 1
- norm_gain: float32 [8, 2048], P('section'), may hold values from 0.5 to 1.5
- router_weight: bfloat16 [8, 2048, 16], P('section'), may hold values from -0.25 to 0.25
- gate_weight: bfloat16 [8, 2048, 12288], P('section', None, 'expert'), may hold values from -0.125 to 0.125
- up_weight: bfloat16 [8, 2048, 12288], P('section', None, 'expert'), may hold values from -0.125 to 0.125
- down_weight: bfloat16 [8, 12288, 2048], P('section', 'expert'), may hold values from -0.21875 to 0.21875
Outputs:
- section_output: bfloat16 [8, 6144, 2048], P('section', 'expert')
- grad_output: bfloat16 [8, 6144, 2048], P('section', 'expert')
Inputs may be any that keep to these rules, and one draw needn't show every extreme that they name: `expert_ids`: each token names 2 different experts. Among the 96 tokens that one index of expert holds for one section and micro-batch, no expert is named more than 16 times, a bound that some block reaches in some of them.
All inputs are finite; a program needn't handle non-finite values. No bound on the sum of `keep_mask` on one device may be relied on, other than what follows from the above.
Results may differ from a plain program's by a relative error of at most 0.012.
Values may be sent and summed in bfloat16 or wider, within the bound.
No kernel may reach another device: no remote copies, remote signals or barrier semaphores. Data moves between devices by JAX's collectives and lax.ppermute only.
A program may use at most 64 MiB of HBM per device.

v0:
```python
import jax
import jax.numpy as jnp
from jax import lax
from jax.experimental import pallas as pl
from jax.experimental.pallas import tpu as pltpu
from jax.sharding import PartitionSpec as P

EPS = 1e-06
KEEP_SCALE = 8.0 / 7.0
NEAR_SETS = ((0, 2, 5, 7), (1, 3, 4, 6))
F32 = jnp.float32
BF16 = jnp.bfloat16
MIB = 1 << 20


def place(x, z, core):
    return (x * 8 + z) * 2 + core


def chips():
    return [(x, z, core) for x in range(4) for z in range(8) for core in range(2)]


def trade_groups():
    return [
        [place(x, z, core) for x in range(4) for z in zs]
        for zs in NEAR_SETS
        for core in range(2)
    ]


def z_partners():
    return [(place(x, z, c), place(x, z ^ 1, c)) for x, z, c in chips()]


def core_partners():
    return [(place(x, z, c), place(x, z, c ^ 1)) for x, z, c in chips()]


def shifted(block, distance):
    n = lax.axis_size("section")
    return lax.ppermute(block, "section", [((i - distance) % n, i) for i in range(n)])


def nt_dot(left, right):
    return lax.dot_general(
        left, right, (((1,), (1,)), ((), ())), preferred_element_type=F32
    )


def tn_dot(left, right):
    return lax.dot_general(
        left, right, (((0,), (0,)), ((), ())), preferred_element_type=F32
    )


def whole(shape):
    return pl.BlockSpec(shape, lambda *_: (0,) * len(shape))


def as_column(row):
    n = row.shape[1]
    eye = lax.broadcasted_iota(jnp.int32, (n, n), 0) == lax.broadcasted_iota(
        jnp.int32, (n, n), 1
    )
    return jnp.sum(jnp.where(eye, row, 0.0), axis=1, keepdims=True)


def prepare(hidden, gain, router_t, ids, keep, sel_ref, col_ref):
    tokens = hidden.shape[0]
    experts = router_t.shape[0]
    slots = sel_ref.shape[1]
    per = slots // experts
    plain = hidden.astype(F32)
    inverse = lax.rsqrt(jnp.mean(plain * plain, axis=-1, keepdims=True) + EPS)
    normed = (plain * inverse * gain).astype(BF16)
    logits = nt_dot(router_t, normed)
    expert_row = lax.broadcasted_iota(jnp.int32, (experts, tokens), 0)
    picked = [
        jnp.sum(jnp.where(expert_row == ids[k], logits, 0.0), axis=0, keepdims=True)
        for k in range(2)
    ]
    probs = [1.0 / (1.0 + jnp.exp(picked[1 - k] - picked[k])) for k in range(2)]
    slot = lax.broadcasted_iota(jnp.int32, (slots, tokens), 0)
    slot_expert = slot // per
    slot_rank = slot % per
    named = [slot_expert == ids[k] for k in range(2)]
    named_any = (named[0] | named[1]).astype(F32).astype(BF16)
    earlier = (
        lax.broadcasted_iota(jnp.int32, (tokens, tokens), 0)
        < lax.broadcasted_iota(jnp.int32, (tokens, tokens), 1)
    ).astype(F32).astype(BF16)
    rank = jnp.dot(named_any, earlier, preferred_element_type=F32)
    here = rank == slot_rank.astype(F32)
    sel = [(named[k] & here).astype(F32).astype(BF16) for k in range(2)]
    sel_ref[0] = sel[0]
    sel_ref[1] = sel[1]
    lane = lax.broadcasted_iota(jnp.int32, (tokens, 128), 1)
    kept = [keep[k].astype(F32) * KEEP_SCALE for k in range(2)]
    rows = [
        kept[0] * probs[0],
        kept[1] * probs[1],
        probs[0],
        probs[1],
        kept[0],
        kept[1],
        ids[0].astype(F32),
        ids[1].astype(F32),
    ]
    cols = jnp.zeros((tokens, 128), F32)
    for at, row in enumerate(rows):
        cols = jnp.where(lane == at, as_column(row), cols)
    col_ref[...] = jnp.where(lane == len(rows), inverse, cols)
    return normed, sel[0] + sel[1]


def prologue_kernel(
    fwd_ref, bwd_ref, up_ref, ids_ref, keep_ref, gain_ref, router_ref,
    send_ref, fsel_ref, fcol_ref, bsel_ref, bcol_ref,
):
    width = fwd_ref.shape[1]
    gain = gain_ref[...]
    router_t = router_ref[...]
    ids = [[ids_ref[m, k : k + 1, :] for k in range(2)] for m in range(2)]
    keep = [[keep_ref[m, k : k + 1, :] for k in range(2)] for m in range(2)]
    normed, sel = prepare(fwd_ref[...], gain, router_t, ids[0], keep[0], fsel_ref, fcol_ref)
    send_ref[:, :width] = jnp.dot(sel, normed, preferred_element_type=F32).astype(BF16)
    normed, sel = prepare(bwd_ref[...], gain, router_t, ids[1], keep[1], bsel_ref, bcol_ref)
    send_ref[:, width : 2 * width] = jnp.dot(
        sel, normed, preferred_element_type=F32
    ).astype(BF16)
    send_ref[:, 2 * width :] = jnp.dot(
        sel, up_ref[...], preferred_element_type=F32
    ).astype(BF16)


def prologue(fwd, bwd, upstream, ids, keep, gain, router_t, slots):
    tokens, width = fwd.shape
    sel = jax.ShapeDtypeStruct((2, slots, tokens), BF16)
    col = jax.ShapeDtypeStruct((tokens, 128), F32)
    outs = (jax.ShapeDtypeStruct((slots, 3 * width), BF16), sel, col, sel, col)
    args = (fwd, bwd, upstream, ids, keep, gain, router_t)
    return pl.pallas_call(
        prologue_kernel,
        out_shape=outs,
        grid=(1,),
        in_specs=[whole(a.shape) for a in args],
        out_specs=[whole(o.shape) for o in outs],
        compiler_params=pltpu.CompilerParams(vmem_limit_bytes=40 * MIB),
        cost_estimate=pl.CostEstimate(
            flops=6 * slots * tokens * width, bytes_accessed=5 * MIB, transcendentals=0
        ),
        name="prologue",
    )(*args)


def fetch(pieces, full, sems, first):
    rows = pieces[0].shape[0]
    copies = []
    for q, piece in enumerate(pieces):
        copy = pltpu.make_async_copy(
            piece, full.at[pl.ds(q * rows, rows)], sems.at[first + q]
        )
        copy.start()
        copies.append(copy)
    return copies


def forward_kernel(rows_ref, *rest):
    pieces = rest[:12]
    out_ref, gate, up, down, act, sems = rest[12:]
    gates = fetch(pieces[0:4], gate, sems, 0)
    ups = fetch(pieces[4:8], up, sems, 4)
    downs = fetch(pieces[8:12], down, sems, 8)
    rows = rows_ref[...]
    hidden = gate.shape[0]
    part = 256
    for at in range(0, hidden, part):
        for q in ((0, 1), (2,), (3,))[at // part]:
            gates[q].wait()
            ups[q].wait()
        pre_gate = nt_dot(rows, gate[at : at + part, :])
        pre_up = nt_dot(rows, up[at : at + part, :])
        act[:, at : at + part] = (
            pre_gate * jax.nn.sigmoid(pre_gate) * pre_up
        ).astype(BF16)
    for copy in downs:
        copy.wait()
    width = down.shape[1]
    step = 512
    for at in range(0, width, step):
        out_ref[:, at : at + step] = jnp.dot(
            act[...], down[:, at : at + step], preferred_element_type=F32
        ).astype(BF16)


def backward_kernel(rows_ref, upstream_ref, *rest):
    pieces = rest[:12]
    out_ref, gate, up, down, grad_gate, grad_up, sems = rest[12:]
    gates = fetch(pieces[0:4], gate, sems, 0)
    ups = fetch(pieces[4:8], up, sems, 4)
    downs = fetch(pieces[8:12], down, sems, 8)
    rows = rows_ref[...]
    upstream = upstream_ref[...]
    hidden = gate.shape[0]
    part = 256
    change = jnp.zeros((rows.shape[0], 1), F32)
    for at in range(0, hidden, part):
        for q in ((0, 1), (2,), (3,))[at // part]:
            gates[q].wait()
            ups[q].wait()
            downs[q].wait()
        pre_gate = nt_dot(rows, gate[at : at + part, :])
        pre_up = nt_dot(rows, up[at : at + part, :])
        pulled = nt_dot(upstream, down[at : at + part, :])
        sigma = jax.nn.sigmoid(pre_gate)
        inner = (pre_gate * sigma * pre_up).astype(BF16).astype(F32)
        change = change + jnp.sum(inner * pulled, axis=1, keepdims=True)
        grad_gate[:, at : at + part] = (
            pulled * pre_up * sigma * (1.0 + pre_gate * (1.0 - sigma))
        ).astype(BF16)
        grad_up[:, at : at + part] = (pulled * pre_gate * sigma).astype(BF16)
    width = gate.shape[1]
    step = 512
    for at in range(0, width, step):
        out_ref[:, at : at + step] = (
            jnp.dot(grad_gate[...], gate[:, at : at + step], preferred_element_type=F32)
            + jnp.dot(grad_up[...], up[:, at : at + step], preferred_element_type=F32)
        ).astype(BF16)
    out_ref[:, width:] = jnp.broadcast_to(change, (rows.shape[0], 128)).astype(BF16)


def expert_call(kernel, got, columns, extra, n_scratch, pieces, name):
    slots = got.shape[0]
    quarter, width = pieces[0].shape
    hidden = 4 * quarter
    full = pltpu.VMEM((hidden, width), BF16)
    return pl.pallas_call(
        kernel,
        out_shape=jax.ShapeDtypeStruct((slots, width + extra), BF16),
        grid=(1,),
        in_specs=[
            pl.BlockSpec((slots, width), lambda i, c=c: (0, c)) for c in columns
        ]
        + [pl.BlockSpec(memory_space=pltpu.HBM)] * 12,
        out_specs=whole((slots, width + extra)),
        scratch_shapes=[full, full, full]
        + [pltpu.VMEM((slots, hidden), BF16)] * n_scratch
        + [pltpu.SemaphoreType.DMA((12,))],
        compiler_params=pltpu.CompilerParams(vmem_limit_bytes=40 * MIB),
        cost_estimate=pl.CostEstimate(
            flops=2 * (2 * n_scratch + 1) * slots * width * hidden,
            bytes_accessed=12 * MIB,
            transcendentals=0,
        ),
        name=name,
    )(
        *[got for _ in columns],
        *[pltpu.with_memory_space_constraint(p, pltpu.HBM) for p in pieces],
    )


def forward_end_kernel(back_ref, sel_ref, col_ref, input_ref, out_ref):
    cols = col_ref[...]
    back = back_ref[...]
    mixed = cols[:, 0:1] * tn_dot(sel_ref[0], back)
    mixed = mixed + cols[:, 1:2] * tn_dot(sel_ref[1], back)
    out_ref[...] = (input_ref[...].astype(F32) + mixed).astype(BF16)


def backward_end_kernel(
    back_ref, sel_ref, col_ref, saved_ref, upstream_ref, gain_ref, router_ref, out_ref
):
    cols = col_ref[...]
    width = saved_ref.shape[1]
    experts = router_ref.shape[0]
    back = back_ref[:, :width]
    tail = back_ref[:, width:]
    change = [
        cols[:, 4 + k : 5 + k] * tn_dot(sel_ref[k], tail)[:, 0:1] for k in range(2)
    ]
    probs = [cols[:, 2 + k : 3 + k] for k in range(2)]
    centre = probs[0] * change[0] + probs[1] * change[1]
    lane = lax.broadcasted_iota(jnp.int32, (cols.shape[0], experts), 1).astype(F32)
    dense = jnp.zeros((cols.shape[0], experts), F32)
    for k in range(2):
        dense = dense + jnp.where(
            lane == cols[:, 6 + k : 7 + k], probs[k] * (change[k] - centre), 0.0
        )
    router_t = router_ref[...]
    total = jnp.zeros((cols.shape[0], width), F32)
    rest = dense
    for _ in range(3):
        term = rest.astype(BF16)
        rest = rest - term.astype(F32)
        total = total + jnp.dot(term, router_t, preferred_element_type=F32)
    for k in range(2):
        total = total + cols[:, k : k + 1] * tn_dot(sel_ref[k], back)
    plain = saved_ref[...].astype(F32)
    inverse = cols[:, 8:9]
    weighted = total * gain_ref[...]
    inner_mean = jnp.mean(weighted * plain, axis=-1, keepdims=True)
    norm_grad = inverse * (weighted - plain * inverse * inverse * inner_mean)
    out_ref[...] = (upstream_ref[...].astype(F32) + norm_grad).astype(BF16)


def end_call(kernel, args, like, name):
    return pl.pallas_call(
        kernel,
        out_shape=jax.ShapeDtypeStruct(like.shape, BF16),
        grid=(1,),
        in_specs=[whole(a.shape) for a in args],
        out_specs=whole(like.shape),
        compiler_params=pltpu.CompilerParams(vmem_limit_bytes=40 * MIB),
        cost_estimate=pl.CostEstimate(
            flops=4 * args[0].shape[0] * like.shape[0] * like.shape[1],
            bytes_accessed=3 * MIB,
            transcendentals=0,
        ),
        name=name,
    )(*args)


def trade(rows):
    groups = trade_groups()
    count = len(groups[0])
    blocks = rows.reshape(count, rows.shape[0] // count, rows.shape[1])
    blocks = lax.all_to_all(
        blocks, "expert", 0, 0, axis_index_groups=groups, tiled=True
    )
    return blocks.reshape(rows.shape)


def on_device(
    section_input,
    saved_input,
    grad_input,
    expert_ids,
    keep_mask,
    norm_gain,
    router_weight,
    gate_weight,
    up_weight,
    down_weight,
):
    own = (gate_weight[0].T, up_weight[0].T, down_weight[0])
    far = [lax.ppermute(w, "expert", z_partners()) for w in own]
    near = [lax.ppermute(w, "expert", core_partners()) for w in own]
    cross = [lax.ppermute(w, "expert", core_partners()) for w in far]
    pieces = [w for four in zip(own, near, far, cross) for w in four]
    ids = expert_ids[0].transpose(0, 2, 1)
    keep = keep_mask[0].transpose(0, 2, 1)
    router_t = router_weight[0].T
    experts = router_t.shape[0]
    slots = experts * 16
    send, fsel, fcol, bsel, bcol = prologue(
        section_input[0], saved_input[0], grad_input[0], ids, keep, norm_gain, router_t, slots
    )
    got = trade(send)
    out_f = expert_call(forward_kernel, got, (0,), 0, 1, pieces, "forward_rows")
    back_f = trade(out_f)
    out_b = expert_call(backward_kernel, got, (1, 2), 128, 2, pieces, "backward_rows")
    back_b = trade(out_b)
    mixed = end_call(
        forward_end_kernel, (back_f, fsel, fcol, section_input[0]), section_input[0], "forward_end"
    )
    input_grad = end_call(
        backward_end_kernel,
        (back_b, bsel, bcol, saved_input[0], grad_input[0], norm_gain, router_t),
        saved_input[0],
        "backward_end",
    )
    return (shifted(mixed, 1)[None], shifted(input_grad, -1)[None])


def solution(mesh):
    return jax.shard_map(
        on_device,
        mesh=mesh,
        in_specs=(
            P("section", "expert", None),
            P("section", "expert", None),
            P("section", "expert", None),
            P("section", None, "expert", None),
            P("section", None, "expert", None),
            P("section", None),
            P("section", None, None),
            P("section", None, "expert"),
            P("section", None, "expert"),
            P("section", "expert", None),
        ),
        out_specs=(P("section", "expert", None), P("section", "expert", None)),
        check_vma=False,
    )
```

profile of v0, /device:TPU:1, one launch (start us, length us, event | category | flops | bytes accessed | tf_op | source)
XLA Modules:
  0.0 234.2 jit_solution(3139597468544399985)
XLA Ops:
  0.6 0.0 copy-start.3
  0.6 1.0 copy-done.3
  1.6 1.0 copy-done.5
  2.6 1.0 copy-done.7
  3.6 0.8 copy-done.9
  4.5 0.7 copy-done.19
  5.2 0.7 copy-done.21
  5.8 0.7 copy-done.22
  6.5 1.5 prologue.1
  8.0 0.0 copy-start.2
  8.0 1.6 copy-done.2
  9.7 0.7 copy-done.11
  10.3 0.7 copy-done.13
  11.0 0.6 copy-done.15
  11.6 0.6 copy-done.17
  12.2 13.4 %all-to-all-start = ((bf16[16,16,6144]{2,1,0:T(8,128)(2,1)}), bf16[16,16,6144]{2,1,0:T(8,128)(2,1)S(1)}, u32[]{:S(2)}, u32[]{:S(2)}) async-start(bf16[16,16,6144]{2,1,0:T(8,128)(2,1)} %bitcast.33), calls=%async_computation | async-start | bytes 6291456 | tf_op jit(solution)/shard_map/all_to_all | solution.py:328
  25.6 2.9 %collective-permute-start = (bf16[192,2048]{1,0:T(8,128)(2,1)}, bf16[192,2048]{1,0:T(8,128)(2,1)S(1)}, u32[]{:S(2)}, u32[]{:S(2)}) collective-permute-start(bf16[192,2048]{1,0:T(8,128)(2,1)} %bitcast.44), channel_id=1, source_target_pairs={{0,1},{1,0},{2,3},{3,2},{4,5},{5,4},{6,7},{7,6},{8,9},{9,8},{10,11... | collective-permute-start | bytes 2359304 | tf_op jit(solution)/shard_map/ppermute | solution.py:348
  28.5 3.1 %collective-permute-start.1 = (bf16[192,2048]{1,0:T(8,128)(2,1)}, bf16[192,2048]{1,0:T(8,128)(2,1)S(1)}, u32[]{:S(2)}, u32[]{:S(2)}) collective-permute-start(bf16[192,2048]{1,0:T(8,128)(2,1)} %bitcast.45), channel_id=1, source_target_pairs={{0,2},{1,3},{2,0},{3,1},{4,6},{5,7},{6,4},{7,5},{8,10},{9,11},{10,... | collective-permute-start | bytes 2359304 | tf_op jit(solution)/shard_map/ppermute | solution.py:347
  31.6 2.2 collective-permute-start.4
  33.8 3.1 %collective-permute-start.7 = (bf16[192,2048]{1,0:T(8,128)(2,1)}, bf16[192,2048]{1,0:T(8,128)(2,1)S(1)}, u32[]{:S(2)}, u32[]{:S(2)}) collective-permute-start(bf16[192,2048]{1,0:T(8,128)(2,1)} %bitcast.52), channel_id=1, source_target_pairs={{0,2},{1,3},{2,0},{3,1},{4,6},{5,7},{6,4},{7,5},{8,10},{9,11},{10,... | collective-permute-start | bytes 2359304 | tf_op jit(solution)/shard_map/ppermute | solution.py:347
  36.9 2.8 %collective-permute-start.3 = (bf16[192,2048]{1,0:T(8,128)(2,1)}, bf16[192,2048]{1,0:T(8,128)(2,1)S(1)}, u32[]{:S(2)}, u32[]{:S(2)}) collective-permute-start(bf16[192,2048]{1,0:T(8,128)(2,1)} %bitcast.49), channel_id=1, source_target_pairs={{0,1},{1,0},{2,3},{3,2},{4,5},{5,4},{6,7},{7,6},{8,9},{9,8},{10,11... | collective-permute-start | bytes 2359304 | tf_op jit(solution)/shard_map/ppermute | solution.py:348
  39.7 0.0 collective-permute-done.rest_1_
  39.7 0.0 copy-start.23
  39.7 1.9 collective-permute-start.6
  41.6 47.8 %collective-permute-done.1.rest_2_ = bf16[192,2048]{1,0:T(8,128)(2,1)S(1)} collective-permute-done((bf16[192,2048]{1,0:T(8,128)(2,1)}, bf16[192,2048]{1,0:T(8,128)(2,1)S(1)}, u32[]{:S(2)}, u32[]{:S(2)}) %collective-permute-start.1) | collective-permute-done | bytes 786464 | tf_op jit(solution)/shard_map/ppermute | solution.py:347
  89.4 9.6 %collective-permute-start.2 = (bf16[192,2048]{1,0:T(8,128)(2,1)S(1)}, bf16[192,2048]{1,0:T(8,128)(2,1)S(1)}, u32[]{:S(2)}, u32[]{:S(2)}) collective-permute-start(bf16[192,2048]{1,0:T(8,128)(2,1)S(1)} %collective-permute-done.1.rest_2_), channel_id=1, source_target_pairs={{0,1},{1,0},{2,3},{3,2},{4,5},{5,4},{6,7},{7,6},{8,9},{9,8},{10,11... | collective-permute-start | bytes 2359304 | tf_op jit(solution)/shard_map/ppermute | solution.py:349
  99.1 12.3 %collective-permute-done.4.rest_6_ = bf16[192,2048]{1,0:T(8,128)(2,1)S(1)} collective-permute-done((bf16[192,2048]{1,0:T(8,128)(2,1)}, bf16[192,2048]{1,0:T(8,128)(2,1)S(1)}, u32[]{:S(2)}, u32[]{:S(2)}) %collective-permute-start.4) | collective-permute-done | bytes 786464 | tf_op jit(solution)/shard_map/ppermute | solution.py:347
  111.4 4.5 %collective-permute-start.5 = (bf16[192,2048]{1,0:T(8,128)(2,1)S(1)}, bf16[192,2048]{1,0:T(8,128)(2,1)S(1)}, u32[]{:S(2)}, u32[]{:S(2)}) collective-permute-start(bf16[192,2048]{1,0:T(8,128)(2,1)S(1)} %collective-permute-done.4.rest_6_), channel_id=1, source_target_pairs={{0,1},{1,0},{2,3},{3,2},{4,5},{5,4},{6,7},{7,6},{8,9},{9,8},{10,11... | collective-permute-start | bytes 2359304 | tf_op jit(solution)/shard_map/ppermute | solution.py:349
  115.9 12.3 %collective-permute-done.7.rest_10_ = bf16[192,2048]{1,0:T(8,128)(2,1)S(1)} collective-permute-done((bf16[192,2048]{1,0:T(8,128)(2,1)}, bf16[192,2048]{1,0:T(8,128)(2,1)S(1)}, u32[]{:S(2)}, u32[]{:S(2)}) %collective-permute-start.7) | collective-permute-done | bytes 786464 | tf_op jit(solution)/shard_map/ppermute | solution.py:347
  128.3 3.4 %collective-permute-start.8 = (bf16[192,2048]{1,0:T(8,128)(2,1)S(1)}, bf16[192,2048]{1,0:T(8,128)(2,1)}, u32[]{:S(2)}, u32[]{:S(2)}) collective-permute-start(bf16[192,2048]{1,0:T(8,128)(2,1)S(1)} %collective-permute-done.7.rest_10_), channel_id=1, source_target_pairs={{0,1},{1,0},{2,3},{3,2},{4,5},{5,4},{6,7},{7,6},{8,9},{9,8},{10,11... | collective-permute-start | bytes 2359304 | tf_op jit(solution)/shard_map/ppermute | solution.py:349
  131.7 0.0 collective-permute-done.3.rest_5_
  131.7 0.0 collective-permute-done.6.rest_9_
  131.7 0.0 collective-permute-done.2.rest_3_
  131.8 0.0 copy-start.29
  131.8 0.0 collective-permute-done.5.rest_7_
  131.8 0.8 copy-done.27
  132.6 0.3 copy-done.28
  133.0 0.2 copy-done.29
  133.2 1.0 copy-done.30
  134.1 0.0 collective-permute-done.8.rest_11_
  134.1 0.0 all-to-all-done
  134.1 5.7 %forward_rows.1 = bf16[256,2048]{1,0:T(8,128)(2,1)S(1)} custom-call(bf16[256,6144]{1,0:T(8,128)(2,1)S(1)} %bitcast.27, bf16[192,2048]{1,0:T(8,128)(2,1)} %bitcast.46, bf16[192,2048]{1,0:T(8,128)(2,1)} %copy-done.23, bf16[192,2048]{1,0:T(8,128)(2,1)} %copy-done.24, bf16[192,2048]{1,0:T(8,128)(2,1)} %copy-done.29, bf16[192,2048]{1,0:T(8,128)(2,1)} %bitcast.50, ...), custom_call_target="tpu_custom_call" | custom-call | flops 2415919104 | bytes 12582912 | tf_op jit(solution)/shard_map/forward_rows/pallas_call | solution.py:238
  139.8 1.0 copy-done.1
  140.8 11.1 %all-to-all-start.1 = ((bf16[16,16,2048]{2,1,0:T(8,128)(2,1)}), bf16[16,16,2048]{2,1,0:T(8,128)(2,1)}, u32[]{:S(2)}, u32[]{:S(2)}) async-start(bf16[16,16,2048]{2,1,0:T(8,128)(2,1)} %bitcast.32), calls=%async_computation.1 | async-start | bytes 2097152 | tf_op jit(solution)/shard_map/all_to_all | solution.py:328
  151.9 0.0 copy-start.8
  151.9 8.9 %backward_rows.1 = bf16[256,2176]{1,0:T(8,128)(2,1)S(1)} custom-call(bf16[256,6144]{1,0:T(8,128)(2,1)S(1)} %bitcast.28, bf16[256,6144]{1,0:T(8,128)(2,1)S(1)} %bitcast.29, bf16[192,2048]{1,0:T(8,128)(2,1)} %bitcast.47, bf16[192,2048]{1,0:T(8,128)(2,1)} %copy-done.23, bf16[192,2048]{1,0:T(8,128)(2,1)} %copy-done.24, bf16[192,2048]{1,0:T(8,128)(2,1)} %copy-done.29, ...), custom_call_target="tpu_custom_call" | custom-call | flops 4026531840 | bytes 12582912 | tf_op jit(solution)/shard_map/backward_rows/pallas_call | solution.py:238
  160.9 1.0 copy-done
  161.9 0.0 copy-start.16
  161.9 0.0 copy-start.20
  161.9 21.2 %all-to-all-done.1 = bf16[16,16,2048]{2,1,0:T(8,128)(2,1)} async-done(((bf16[16,16,2048]{2,1,0:T(8,128)(2,1)}), bf16[16,16,2048]{2,1,0:T(8,128)(2,1)}, u32[]{:S(2)}, u32[]{:S(2)}) %all-to-all-start.1) | async-done | bytes 1048608 | tf_op jit(solution)/shard_map/all_to_all | solution.py:328
  183.1 3.7 %all-to-all-start.2 = ((bf16[16,16,2176]{2,1,0:T(8,128)(2,1)}), bf16[16,16,2176]{2,1,0:T(8,128)(2,1)S(1)}, u32[]{:S(2)}, u32[]{:S(2)}) async-start(bf16[16,16,2176]{2,1,0:T(8,128)(2,1)} %bitcast.30), calls=%async_computation.2 | async-start | bytes 2228224 | tf_op jit(solution)/shard_map/all_to_all | solution.py:328
  186.8 0.0 copy-start.14
  186.8 0.9 copy-done.14
  187.7 0.8 copy-done.18
  188.5 1.7 forward_end.1
  190.3 3.2 %collective-permute-start.9 = (bf16[96,2048]{1,0:T(8,128)(2,1)S(1)}, bf16[96,2048]{1,0:T(8,128)(2,1)S(1)}, u32[]{:S(2)}, u32[]{:S(2)}) collective-permute-start(bf16[96,2048]{1,0:T(8,128)(2,1)S(1)} %forward_end.1), channel_id=1, source_target_pairs={{448,0},{0,64},{64,128},{128,192},{192,256},{256,320},{320,384},{3... | collective-permute-start | bytes 1179656 | tf_op jit(solution)/shard_map/ppermute | solution.py:42
  193.5 24.4 %all-to-all-done.2 = bf16[16,16,2176]{2,1,0:T(8,128)(2,1)S(1)} async-done(((bf16[16,16,2176]{2,1,0:T(8,128)(2,1)}), bf16[16,16,2176]{2,1,0:T(8,128)(2,1)S(1)}, u32[]{:S(2)}, u32[]{:S(2)}) %all-to-all-start.2) | async-done | bytes 1114144 | tf_op jit(solution)/shard_map/all_to_all | solution.py:328
  217.9 0.0 copy-done.4
  217.9 1.7 backward_end.1
  219.6 5.1 %collective-permute-start.10 = (bf16[96,2048]{1,0:T(8,128)(2,1)S(1)}, bf16[96,2048]{1,0:T(8,128)(2,1)S(1)}, u32[]{:S(2)}, u32[]{:S(2)}) collective-permute-start(bf16[96,2048]{1,0:T(8,128)(2,1)S(1)} %backward_end.1), channel_id=1, source_target_pairs={{64,0},{128,64},{192,128},{256,192},{320,256},{384,320},{448,384},... | collective-permute-start | bytes 1179656 | tf_op jit(solution)/shard_map/ppermute | solution.py:42
  224.7 0.0 collective-permute-done.9
  224.7 8.0 %collective-permute-done.10 = bf16[96,2048]{1,0:T(8,128)(2,1)S(1)} collective-permute-done((bf16[96,2048]{1,0:T(8,128)(2,1)S(1)}, bf16[96,2048]{1,0:T(8,128)(2,1)S(1)}, u32[]{:S(2)}, u32[]{:S(2)}) %collective-permute-start.10) | collective-permute-done | bytes 393248 | tf_op jit(solution)/shard_map/ppermute | solution.py:42
  232.7 0.7 copy.14
  233.4 0.7 copy.15
  (33 shorter events, 0.1 us)
Async XLA Ops:
  0.6 1.0 copy-start.3
  1.6 1.0 copy-start.5
  2.6 1.0 copy-start.7
  3.6 0.8 copy-start.9
  4.5 0.7 copy-start.19
  5.2 0.7 copy-start.21
  5.8 0.7 copy-start.22
  8.0 1.6 copy-start.2
  9.7 0.7 copy-start.11
  10.3 0.7 copy-start.13
  11.0 0.6 copy-start.15
  11.6 0.6 copy-start.17
  12.2 121.9 %all-to-all-start = ((bf16[16,16,6144]{2,1,0:T(8,128)(2,1)}), bf16[16,16,6144]{2,1,0:T(8,128)(2,1)S(1)}, u32[]{:S(2)}, u32[]{:S(2)}) async-start(bf16[16,16,6144]{2,1,0:T(8,128)(2,1)} %bitcast.33), calls=%async_computation | async-start | bytes 6291456 | tf_op jit(solution)/shard_map/all_to_all | solution.py:328
  25.6 14.0 %collective-permute-start = (bf16[192,2048]{1,0:T(8,128)(2,1)}, bf16[192,2048]{1,0:T(8,128)(2,1)S(1)}, u32[]{:S(2)}, u32[]{:S(2)}) collective-permute-start(bf16[192,2048]{1,0:T(8,128)(2,1)} %bitcast.44), channel_id=1, source_target_pairs={{0,1},{1,0},{2,3},{3,2},{4,5},{5,4},{6,7},{7,6},{8,9},{9,8},{10,11... | collective-permute-start | bytes 2359304 | tf_op jit(solution)/shard_map/ppermute | solution.py:348
  28.5 60.9 %collective-permute-start.1 = (bf16[192,2048]{1,0:T(8,128)(2,1)}, bf16[192,2048]{1,0:T(8,128)(2,1)S(1)}, u32[]{:S(2)}, u32[]{:S(2)}) collective-permute-start(bf16[192,2048]{1,0:T(8,128)(2,1)} %bitcast.45), channel_id=1, source_target_pairs={{0,2},{1,3},{2,0},{3,1},{4,6},{5,7},{6,4},{7,5},{8,10},{9,11},{10,... | collective-permute-start | bytes 2359304 | tf_op jit(solution)/shard_map/ppermute | solution.py:347
  31.6 79.8 %collective-permute-start.4 = (bf16[192,2048]{1,0:T(8,128)(2,1)}, bf16[192,2048]{1,0:T(8,128)(2,1)S(1)}, u32[]{:S(2)}, u32[]{:S(2)}) collective-permute-start(bf16[192,2048]{1,0:T(8,128)(2,1)} %bitcast.48), channel_id=1, source_target_pairs={{0,2},{1,3},{2,0},{3,1},{4,6},{5,7},{6,4},{7,5},{8,10},{9,11},{10,... | collective-permute-start | bytes 2359304 | tf_op jit(solution)/shard_map/ppermute | solution.py:347
  33.8 94.5 %collective-permute-start.7 = (bf16[192,2048]{1,0:T(8,128)(2,1)}, bf16[192,2048]{1,0:T(8,128)(2,1)S(1)}, u32[]{:S(2)}, u32[]{:S(2)}) collective-permute-start(bf16[192,2048]{1,0:T(8,128)(2,1)} %bitcast.52), channel_id=1, source_target_pairs={{0,2},{1,3},{2,0},{3,1},{4,6},{5,7},{6,4},{7,5},{8,10},{9,11},{10,... | collective-permute-start | bytes 2359304 | tf_op jit(solution)/shard_map/ppermute | solution.py:347
  36.9 94.8 %collective-permute-start.3 = (bf16[192,2048]{1,0:T(8,128)(2,1)}, bf16[192,2048]{1,0:T(8,128)(2,1)S(1)}, u32[]{:S(2)}, u32[]{:S(2)}) collective-permute-start(bf16[192,2048]{1,0:T(8,128)(2,1)} %bitcast.49), channel_id=1, source_target_pairs={{0,1},{1,0},{2,3},{3,2},{4,5},{5,4},{6,7},{7,6},{8,9},{9,8},{10,11... | collective-permute-start | bytes 2359304 | tf_op jit(solution)/shard_map/ppermute | solution.py:348
  39.7 92.1 %copy-start.23 = (bf16[192,2048]{1,0:T(8,128)(2,1)}, bf16[192,2048]{1,0:T(8,128)(2,1)S(1)}, u32[]{:S(2)}) copy-start(bf16[192,2048]{1,0:T(8,128)(2,1)S(1)} %collective-permute-done.rest_1_) | copy-start | bytes 2359300
  39.7 92.0 %collective-permute-start.6 = (bf16[192,2048]{1,0:T(8,128)(2,1)}, bf16[192,2048]{1,0:T(8,128)(2,1)S(1)}, u32[]{:S(2)}, u32[]{:S(2)}) collective-permute-start(bf16[192,2048]{1,0:T(8,128)(2,1)} %bitcast.53), channel_id=1, source_target_pairs={{0,1},{1,0},{2,3},{3,2},{4,5},{5,4},{6,7},{7,6},{8,9},{9,8},{10,11... | collective-permute-start | bytes 2359304 | tf_op jit(solution)/shard_map/ppermute | solution.py:348
  89.4 42.3 %copy-start.24 = (bf16[192,2048]{1,0:T(8,128)(2,1)}, bf16[192,2048]{1,0:T(8,128)(2,1)S(1)}, u32[]{:S(2)}) copy-start(bf16[192,2048]{1,0:T(8,128)(2,1)S(1)} %collective-permute-done.1.rest_2_) | copy-start | bytes 2359300
  89.4 42.3 %collective-permute-start.2 = (bf16[192,2048]{1,0:T(8,128)(2,1)S(1)}, bf16[192,2048]{1,0:T(8,128)(2,1)S(1)}, u32[]{:S(2)}, u32[]{:S(2)}) collective-permute-start(bf16[192,2048]{1,0:T(8,128)(2,1)S(1)} %collective-permute-done.1.rest_2_), channel_id=1, source_target_pairs={{0,1},{1,0},{2,3},{3,2},{4,5},{5,4},{6,7},{7,6},{8,9},{9,8},{10,11... | collective-permute-start | bytes 2359304 | tf_op jit(solution)/shard_map/ppermute | solution.py:349
  111.4 20.4 %copy-start.25 = (bf16[192,2048]{1,0:T(8,128)(2,1)}, bf16[192,2048]{1,0:T(8,128)(2,1)S(1)}, u32[]{:S(2)}) copy-start(bf16[192,2048]{1,0:T(8,128)(2,1)S(1)} %collective-permute-done.4.rest_6_) | copy-start | bytes 2359300
  111.4 20.3 %collective-permute-start.5 = (bf16[192,2048]{1,0:T(8,128)(2,1)S(1)}, bf16[192,2048]{1,0:T(8,128)(2,1)S(1)}, u32[]{:S(2)}, u32[]{:S(2)}) collective-permute-start(bf16[192,2048]{1,0:T(8,128)(2,1)S(1)} %collective-permute-done.4.rest_6_), channel_id=1, source_target_pairs={{0,1},{1,0},{2,3},{3,2},{4,5},{5,4},{6,7},{7,6},{8,9},{9,8},{10,11... | collective-permute-start | bytes 2359304 | tf_op jit(solution)/shard_map/ppermute | solution.py:349
  128.3 3.5 %copy-start.26 = (bf16[192,2048]{1,0:T(8,128)(2,1)}, bf16[192,2048]{1,0:T(8,128)(2,1)S(1)}, u32[]{:S(2)}) copy-start(bf16[192,2048]{1,0:T(8,128)(2,1)S(1)} %collective-permute-done.7.rest_10_) | copy-start | bytes 2359300
  128.3 5.9 %collective-permute-start.8 = (bf16[192,2048]{1,0:T(8,128)(2,1)S(1)}, bf16[192,2048]{1,0:T(8,128)(2,1)}, u32[]{:S(2)}, u32[]{:S(2)}) collective-permute-start(bf16[192,2048]{1,0:T(8,128)(2,1)S(1)} %collective-permute-done.7.rest_10_), channel_id=1, source_target_pairs={{0,1},{1,0},{2,3},{3,2},{4,5},{5,4},{6,7},{7,6},{8,9},{9,8},{10,11... | collective-permute-start | bytes 2359304 | tf_op jit(solution)/shard_map/ppermute | solution.py:349
  131.7 0.9 copy-start.27
  131.7 1.2 copy-start.28
  131.8 1.4 copy-start.29
  133.2 1.0 copy-start.30
  139.8 1.0 copy-start.1
  140.8 42.3 %all-to-all-start.1 = ((bf16[16,16,2048]{2,1,0:T(8,128)(2,1)}), bf16[16,16,2048]{2,1,0:T(8,128)(2,1)}, u32[]{:S(2)}, u32[]{:S(2)}) async-start(bf16[16,16,2048]{2,1,0:T(8,128)(2,1)} %bitcast.32), calls=%async_computation.1 | async-start | bytes 2097152 | tf_op jit(solution)/shard_map/all_to_all | solution.py:328
  151.9 34.9 %copy-start.8 = (bf16[1,96,2048]{2,1,0:T(8,128)(2,1)S(1)}, bf16[1,96,2048]{2,1,0:T(8,128)(2,1)}, u32[]{:S(2)}) copy-start(bf16[1,96,2048]{2,1,0:T(8,128)(2,1)} %param.10) | copy-start | bytes 1179652
  160.9 1.0 copy-start
  161.9 56.0 %copy-start.4 = (bf16[1,96,2048]{2,1,0:T(8,128)(2,1)S(1)}, bf16[1,96,2048]{2,1,0:T(8,128)(2,1)}, u32[]{:S(2)}) copy-start(bf16[1,96,2048]{2,1,0:T(8,128)(2,1)} %param.11) | copy-start | bytes 1179652
  161.9 56.0 %copy-start.6 = (bf16[1,96,2048]{2,1,0:T(8,128)(2,1)S(1)}, bf16[1,96,2048]{2,1,0:T(8,128)(2,1)}, u32[]{:S(2)}) copy-start(bf16[1,96,2048]{2,1,0:T(8,128)(2,1)} %param.12) | copy-start | bytes 1179652
  161.9 56.0 %copy-start.10 = (bf16[1,2048,16]{1,2,0:T(8,128)(2,1)S(1)}, bf16[1,2048,16]{1,2,0:T(8,128)(2,1)}, u32[]{:S(2)}) copy-start(bf16[1,2048,16]{1,2,0:T(8,128)(2,1)} %param.16) | copy-start | bytes 196612
  161.9 56.0 %copy-start.12 = (bf16[2,256,96]{2,1,0:T(8,128)(2,1)S(1)}, bf16[2,256,96]{2,1,0:T(8,128)(2,1)}, u32[]{:S(2)}) copy-start(bf16[2,256,96]{2,1,0:T(8,128)(2,1)} %copy-done.11) | copy-start | bytes 294916
  161.9 56.0 %copy-start.16 = (f32[96,128]{1,0:T(8,128)S(1)}, f32[96,128]{1,0:T(8,128)}, u32[]{:S(2)}) copy-start(f32[96,128]{1,0:T(8,128)} %copy-done.15) | copy-start | bytes 147460
  161.9 56.0 %copy-start.20 = (f32[1,2048]{1,0:T(1,128)S(1)}, f32[1,2048]{1,0:T(1,128)}, u32[]{:S(2)}) copy-start(f32[1,2048]{1,0:T(1,128)} %gain_ref.3) | copy-start | bytes 24580
  183.1 34.8 %all-to-all-start.2 = ((bf16[16,16,2176]{2,1,0:T(8,128)(2,1)}), bf16[16,16,2176]{2,1,0:T(8,128)(2,1)S(1)}, u32[]{:S(2)}, u32[]{:S(2)}) async-start(bf16[16,16,2176]{2,1,0:T(8,128)(2,1)} %bitcast.30), calls=%async_computation.2 | async-start | bytes 2228224 | tf_op jit(solution)/shard_map/all_to_all | solution.py:328
  186.8 0.9 copy-start.14
  187.7 0.8 copy-start.18
  190.3 34.4 %collective-permute-start.9 = (bf16[96,2048]{1,0:T(8,128)(2,1)S(1)}, bf16[96,2048]{1,0:T(8,128)(2,1)S(1)}, u32[]{:S(2)}, u32[]{:S(2)}) collective-permute-start(bf16[96,2048]{1,0:T(8,128)(2,1)S(1)} %forward_end.1), channel_id=1, source_target_pairs={{448,0},{0,64},{64,128},{128,192},{192,256},{256,320},{320,384},{3... | collective-permute-start | bytes 1179656 | tf_op jit(solution)/shard_map/ppermute | solution.py:42
  219.6 13.1 %collective-permute-start.10 = (bf16[96,2048]{1,0:T(8,128)(2,1)S(1)}, bf16[96,2048]{1,0:T(8,128)(2,1)S(1)}, u32[]{:S(2)}, u32[]{:S(2)}) collective-permute-start(bf16[96,2048]{1,0:T(8,128)(2,1)S(1)} %backward_end.1), channel_id=1, source_target_pairs={{64,0},{128,64},{192,128},{256,192},{320,256},{384,320},{448,384},... | collective-permute-start | bytes 1179656 | tf_op jit(solution)/shard_map/ppermute | solution.py:42
where the time goes:
time: 235 us; the launch traced here: 234 us
  waiting for transfers between devices  126 us (54%)
  starting transfers between devices  70 us (30%)
  Pallas kernels  19.5 us (8%)
  local copies, waits for them, and re-layouts  17.6 us (7%)
    ppermute x3, waiting for transfers between devices, on_device(): far = [lax.ppermute(w, 'expert', z_partners()) for w in own]  72.5 us
    all_to_all x3, waiting for transfers between devices, trade(): lax.all_to_all(blocks, 'expert', 0, 0, axis_index_groups=groups, tiled=True)  45.6 us
    all_to_all x3, starting transfers between devices, trade(): lax.all_to_all(blocks, 'expert', 0, 0, axis_index_groups=groups, tiled=True)  28.3 us
    unnamed x64, local copies, waits for them, and re-layouts  17.6 us
    ppermute x3, starting transfers between devices, on_device(): cross = [lax.ppermute(w, 'expert', core_partners()) for w in far]  17.6 us
    pallas_call x2, Pallas kernels, expert_call(): pl.pallas_call(kernel, out_shape=jax.ShapeDtypeStruct((slots, width + ext...  14.6 us
    ppermute x3, starting transfers between devices, on_device(): far = [lax.ppermute(w, 'expert', z_partners()) for w in own]  8.37 us
    ppermute x2, starting transfers between devices, shifted(): lax.ppermute(block, 'section', [((i - distance) % n, i) for i in range(n)])  8.3 us
  transfers between devices with their start and end apart: 14, of which 6 were waited for; matrix products, arithmetic and copies ran while one was open for 0% of the time, Pallas kernels for 5%

commit v1 on v0

--- a/solution.py
+++ b/solution.py
@@ -1,3 +1,5 @@
+import functools
+
 import jax
 import jax.numpy as jnp
 from jax import lax
@@ -114,155 +116,268 @@
     return normed, sel[0] + sel[1]
 
 
+def in_hbm(*arrays):
+    return [pltpu.with_memory_space_constraint(a, pltpu.HBM) for a in arrays]
+
+
+HBM_SPEC = pl.BlockSpec(memory_space=pltpu.HBM)
+
+
+def start_copies(pairs, sems):
+    copies = []
+    for at, (source, target) in enumerate(pairs):
+        copy = pltpu.make_async_copy(source, target, sems.at[at])
+        copy.start()
+        copies.append(copy)
+    return copies
+
+
 def prologue_kernel(
-    fwd_ref, bwd_ref, up_ref, ids_ref, keep_ref, gain_ref, router_ref,
-    send_ref, fsel_ref, fcol_ref, bsel_ref, bcol_ref,
+    fwd_hbm, bwd_hbm, up_hbm, ids_hbm, keep_hbm, gain_hbm, router_hbm,
+    send_hbm, fsel_ref, fcol_ref, bsel_ref, bcol_ref,
+    fwd_ref, bwd_ref, up_ref, ids_ref, keep_ref, gain_ref, router_ref, send_ref, sems,
 ):
     width = fwd_ref.shape[1]
+    loads = start_copies(
+        [
+            (gain_hbm, gain_ref),
+            (router_hbm, router_ref),
+            (ids_hbm, ids_ref),
+            (keep_hbm, keep_ref),
+            (fwd_hbm, fwd_ref),
+            (bwd_hbm, bwd_ref),
+            (up_hbm, up_ref),
+        ],
+        sems,
+    )
+    for load in loads[:5]:
+        load.wait()
     gain = gain_ref[...]
     router_t = router_ref[...]
     ids = [[ids_ref[m, k : k + 1, :] for k in range(2)] for m in range(2)]
     keep = [[keep_ref[m, k : k + 1, :] for k in range(2)] for m in range(2)]
+    stores = []
+
+    def put(place, sel, values):
+        part = pl.ds(place * width, width)
+        send_ref[:, part] = jnp.dot(sel, values, preferred_element_type=F32).astype(BF16)
+        store = pltpu.make_async_copy(
+            send_ref.at[:, part], send_hbm.at[:, part], sems.at[7 + place]
+        )
+        store.start()
+        stores.append(store)
+
     normed, sel = prepare(fwd_ref[...], gain, router_t, ids[0], keep[0], fsel_ref, fcol_ref)
-    send_ref[:, :width] = jnp.dot(sel, normed, preferred_element_type=F32).astype(BF16)
+    put(0, sel, normed)
+    loads[5].wait()
     normed, sel = prepare(bwd_ref[...], gain, router_t, ids[1], keep[1], bsel_ref, bcol_ref)
-    send_ref[:, width : 2 * width] = jnp.dot(
-        sel, normed, preferred_element_type=F32
-    ).astype(BF16)
-    send_ref[:, 2 * width :] = jnp.dot(
-        sel, up_ref[...], preferred_element_type=F32
-    ).astype(BF16)
+    put(1, sel, normed)
+    loads[6].wait()
+    put(2, sel, up_ref[...])
+    for store in stores:
+        store.wait()
 
 
 def prologue(fwd, bwd, upstream, ids, keep, gain, router_t, slots):
     tokens, width = fwd.shape
     sel = jax.ShapeDtypeStruct((2, slots, tokens), BF16)
     col = jax.ShapeDtypeStruct((tokens, 128), F32)
-    outs = (jax.ShapeDtypeStruct((slots, 3 * width), BF16), sel, col, sel, col)
+    vmem = pl.BlockSpec(memory_space=pltpu.VMEM)
     args = (fwd, bwd, upstream, ids, keep, gain, router_t)
     return pl.pallas_call(
         prologue_kernel,
-        out_shape=outs,
-        grid=(1,),
-        in_specs=[whole(a.shape) for a in args],
-        out_specs=[whole(o.shape) for o in outs],
-        compiler_params=pltpu.CompilerParams(vmem_limit_bytes=40 * MIB),
+        out_shape=(pltpu.HBM((slots, 3 * width), BF16), sel, col, sel, col),
+        in_specs=[HBM_SPEC] * len(args),
+        out_specs=[HBM_SPEC] + [vmem] * 4,
+        scratch_shapes=[pltpu.VMEM(a.shape, a.dtype) for a in args]
+        + [pltpu.VMEM((slots, 3 * width), BF16), pltpu.SemaphoreType.DMA((10,))],
+        compiler_params=pltpu.CompilerParams(vmem_limit_bytes=24 * MIB),
         cost_estimate=pl.CostEstimate(
             flops=6 * slots * tokens * width, bytes_accessed=5 * MIB, transcendentals=0
         ),
         name="prologue",
-    )(*args)
-
-
-def fetch(pieces, full, sems, first):
-    rows = pieces[0].shape[0]
-    copies = []
-    for q, piece in enumerate(pieces):
+    )(*in_hbm(*args))
+
+
+def load_pieces(pieces, full, n_pieces):
+    quarter = pieces[0].shape[0]
+    return [
+        (piece, full.at[pl.ds((at % n_pieces) * quarter, quarter)])
+        for at, piece in enumerate(pieces)
+    ]
+
+
+def gate_terms(pre_gate, pre_up):
+    sigma = jax.nn.sigmoid(pre_gate)
+    inner = (pre_gate * sigma * pre_up).astype(BF16)
+    to_gate = pre_up * sigma * (1.0 + pre_gate * (1.0 - sigma))
+    return inner, to_gate, pre_gate * sigma
+
+
+STEP = 512
+
+
+def near_kernel(n, *refs):
+    got_hbm, pieces, refs = refs[0], refs[1 : 1 + 3 * n], refs[1 + 3 * n :]
+    sum_f, sum_b, change_ref, got, gate, up, down, sems = refs
+    width = gate.shape[1]
+    pairs = [(got_hbm, got)]
+    pairs += load_pieces(pieces[:n], gate, n)
+    pairs += load_pieces(pieces[n : 2 * n], up, n)
+    pairs += load_pieces(pieces[2 * n :], down, n)
+    copies = start_copies(pairs, sems)
+    for copy in copies[: 1 + 2 * n]:
+        copy.wait()
+    rows = got[:, :width]
+    act, _, _ = gate_terms(nt_dot(rows, gate[...]), nt_dot(rows, up[...]))
+    for copy in copies[1 + 2 * n :]:
+        copy.wait()
+    for at in range(0, width, STEP):
+        sum_f[:, at : at + STEP] = jnp.dot(
+            act, down[:, at : at + STEP], preferred_element_type=F32
+        )
+    rows = got[:, width : 2 * width]
+    inner, to_gate, to_up = gate_terms(nt_dot(rows, gate[...]), nt_dot(rows, up[...]))
+    pulled = nt_dot(got[:, 2 * width :], down[...])
+    change = jnp.sum(inner.astype(F32) * pulled, axis=1, keepdims=True)
+    change_ref[...] = jnp.broadcast_to(change, change_ref.shape)
+    grad_gate = (pulled * to_gate).astype(BF16)
+    grad_up = (pulled * to_up).astype(BF16)
+    for at in range(0, width, STEP):
+        sum_b[:, at : at + STEP] = jnp.dot(
+            grad_gate, gate[:, at : at + STEP], preferred_element_type=F32
+        ) + jnp.dot(grad_up, up[:, at : at + STEP], preferred_element_type=F32)
+
+
+def front_kernel(n, *refs):
+    got_hbm, pieces, refs = refs[0], refs[1 : 1 + 2 * n], refs[1 + 2 * n :]
+    act_ref, inner_ref, to_gate_ref, to_up_ref, got, gate, up, sems = refs
+    width = gate.shape[1]
+    pairs = [(got_hbm.at[:, pl.ds(0, 2 * width)], got)]
+    pairs += load_pieces(pieces[:n], gate, n)
+    pairs += load_pieces(pieces[n:], up, n)
+    for copy in start_copies(pairs, sems):
+        copy.wait()
+    rows = got[:, :width]
+    act, _, _ = gate_terms(nt_dot(rows, gate[...]), nt_dot(rows, up[...]))
+    act_ref[...] = act
+    rows = got[:, width:]
+    inner, to_gate, to_up = gate_terms(nt_dot(rows, gate[...]), nt_dot(rows, up[...]))
+    inner_ref[...] = inner
+    to_gate_ref[...] = to_gate
+    to_up_ref[...] = to_up
+
+
+def far_kernel(n, *refs):
+    got_hbm, pieces, refs = refs[0], refs[1 : 1 + 3 * n], refs[1 + 3 * n :]
+    sum_f, sum_b, change_ref, act, inner, to_gate, to_up, out_hbm = refs[:8]
+    upstream, gate, up, down, out, sems = refs[8:]
+    width = gate.shape[1]
+    pairs = load_pieces(pieces[2 * n :], down, n)
+    pairs += [(got_hbm.at[:, pl.ds(2 * width, width)], upstream)]
+    pairs += load_pieces(pieces[:n], gate, n)
+    pairs += load_pieces(pieces[n : 2 * n], up, n)
+    copies = start_copies(pairs, sems)
+    stores = []
+
+    def store(at, size):
+        part = pl.ds(at, size)
         copy = pltpu.make_async_copy(
-            piece, full.at[pl.ds(q * rows, rows)], sems.at[first + q]
+            out.at[:, part], out_hbm.at[:, part], sems.at[len(pairs) + len(stores)]
         )
         copy.start()
-        copies.append(copy)
-    return copies
-
-
-def forward_kernel(rows_ref, *rest):
-    pieces = rest[:12]
-    out_ref, gate, up, down, act, sems = rest[12:]
-    gates = fetch(pieces[0:4], gate, sems, 0)
-    ups = fetch(pieces[4:8], up, sems, 4)
-    downs = fetch(pieces[8:12], down, sems, 8)
-    rows = rows_ref[...]
-    hidden = gate.shape[0]
-    part = 256
-    for at in range(0, hidden, part):
-        for q in ((0, 1), (2,), (3,))[at // part]:
-            gates[q].wait()
-            ups[q].wait()
-        pre_gate = nt_dot(rows, gate[at : at + part, :])
-        pre_up = nt_dot(rows, up[at : at + part, :])
-        act[:, at : at + part] = (
-            pre_gate * jax.nn.sigmoid(pre_gate) * pre_up
+        stores.append(copy)
+
+    for copy in copies[: n + 1]:
+        copy.wait()
+    pulled = nt_dot(upstream[...], down[...])
+    change = jnp.sum(inner[...].astype(F32) * pulled, axis=1, keepdims=True)
+    out[:, 2 * width :] = (change_ref[...] + change).astype(BF16)
+    grad_gate = (pulled * to_gate[...]).astype(BF16)
+    grad_up = (pulled * to_up[...]).astype(BF16)
+    for at in range(0, width, STEP):
+        out[:, at : at + STEP] = (
+            sum_f[:, at : at + STEP]
+            + jnp.dot(act[...], down[:, at : at + STEP], preferred_element_type=F32)
         ).astype(BF16)
-    for copy in downs:
+    store(0, width)
+    for copy in copies[n + 1 :]:
         copy.wait()
-    width = down.shape[1]
-    step = 512
-    for at in range(0, width, step):
-        out_ref[:, at : at + step] = jnp.dot(
-            act[...], down[:, at : at + step], preferred_element_type=F32
+    for at in range(0, width, STEP):
+        out[:, width + at : width + at + STEP] = (
+            sum_b[:, at : at + STEP]
+            + jnp.dot(grad_gate, gate[:, at : at + STEP], preferred_element_type=F32)
+            + jnp.dot(grad_up, up[:, at : at + STEP], preferred_element_type=F32)
         ).astype(BF16)
-
-
-def backward_kernel(rows_ref, upstream_ref, *rest):
-    pieces = rest[:12]
-    out_ref, gate, up, down, grad_gate, grad_up, sems = rest[12:]
-    gates = fetch(pieces[0:4], gate, sems, 0)
-    ups = fetch(pieces[4:8], up, sems, 4)
-    downs = fetch(pieces[8:12], down, sems, 8)
-    rows = rows_ref[...]
-    upstream = upstream_ref[...]
-    hidden = gate.shape[0]
-    part = 256
-    change = jnp.zeros((rows.shape[0], 1), F32)
-    for at in range(0, hidden, part):
-        for q in ((0, 1), (2,), (3,))[at // part]:
-            gates[q].wait()
-            ups[q].wait()
-            downs[q].wait()
-        pre_gate = nt_dot(rows, gate[at : at + part, :])
-        pre_up = nt_dot(rows, up[at : at + part, :])
-        pulled = nt_dot(upstream, down[at : at + part, :])
-        sigma = jax.nn.sigmoid(pre_gate)
-        inner = (pre_gate * sigma * pre_up).astype(BF16).astype(F32)
-        change = change + jnp.sum(inner * pulled, axis=1, keepdims=True)
-        grad_gate[:, at : at + part] = (
-            pulled * pre_up * sigma * (1.0 + pre_gate * (1.0 - sigma))
-        ).astype(BF16)
-        grad_up[:, at : at + part] = (pulled * pre_gate * sigma).astype(BF16)
-    width = gate.shape[1]
-    step = 512
-    for at in range(0, width, step):
-        out_ref[:, at : at + step] = (
-            jnp.dot(grad_gate[...], gate[:, at : at + step], preferred_element_type=F32)
-            + jnp.dot(grad_up[...], up[:, at : at + step], preferred_element_type=F32)
-        ).astype(BF16)
-    out_ref[:, width:] = jnp.broadcast_to(change, (rows.shape[0], 128)).astype(BF16)
-
-
-def expert_call(kernel, got, columns, extra, n_scratch, pieces, name):
+    store(width, width + 128)
+    for copy in stores:
+        copy.wait()
+
+
+def expert_calls(got, near_pieces, far_pieces, after_near):
     slots = got.shape[0]
-    quarter, width = pieces[0].shape
-    hidden = 4 * quarter
+    n = 2
+    quarter, width = near_pieces[0].shape
+    hidden = n * quarter
     full = pltpu.VMEM((hidden, width), BF16)
+    vmem = pl.BlockSpec(memory_space=pltpu.VMEM)
+    anywhere = pl.BlockSpec(memory_space=pl.ANY)
+
+    def shape(columns, dtype):
+        return jax.ShapeDtypeStruct((slots, columns), dtype)
+
+    def params(dots, mib):
+        return dict(
+            compiler_params=pltpu.CompilerParams(vmem_limit_bytes=mib * MIB),
+            cost_estimate=pl.CostEstimate(
+                flops=2 * dots * slots * width * hidden,
+                bytes_accessed=8 * MIB,
+                transcendentals=0,
+            ),
+        )
+
+    sums = pl.pallas_call(
+        functools.partial(near_kernel, n),
+        out_shape=[shape(width, F32), shape(width, F32), shape(128, F32)],
+        in_specs=[anywhere] + [HBM_SPEC] * 6,
+        out_specs=[vmem] * 3,
+        scratch_shapes=[pltpu.VMEM(got.shape, BF16), full, full, full]
+        + [pltpu.SemaphoreType.DMA((7,))],
+        name="near_share",
+        **params(8, 32),
+    )(got, *near_pieces)
+    far_pieces, sums = after_near(far_pieces, sums)
+    fronts = pl.pallas_call(
+        functools.partial(front_kernel, n),
+        out_shape=[
+            shape(hidden, BF16),
+            shape(hidden, BF16),
+            shape(hidden, F32),
+            shape(hidden, F32),
+        ],
+        in_specs=[anywhere] + [HBM_SPEC, anywhere] * 2,
+        out_specs=[vmem] * 4,
+        scratch_shapes=[pltpu.VMEM((slots, 2 * width), BF16), full, full]
+        + [pltpu.SemaphoreType.DMA((5,))],
+        name="far_front",
+        **params(4, 24),
+    )(got, *far_pieces[:4])
     return pl.pallas_call(
-        kernel,
-        out_shape=jax.ShapeDtypeStruct((slots, width + extra), BF16),
-        grid=(1,),
-        in_specs=[
-            pl.BlockSpec((slots, width), lambda i, c=c: (0, c)) for c in columns
-        ]
-        + [pl.BlockSpec(memory_space=pltpu.HBM)] * 12,
-        out_specs=whole((slots, width + extra)),
-        scratch_shapes=[full, full, full]
-        + [pltpu.VMEM((slots, hidden), BF16)] * n_scratch
-        + [pltpu.SemaphoreType.DMA((12,))],
-        compiler_params=pltpu.CompilerParams(vmem_limit_bytes=40 * MIB),
-        cost_estimate=pl.CostEstimate(
-            flops=2 * (2 * n_scratch + 1) * slots * width * hidden,
-            bytes_accessed=12 * MIB,
-            transcendentals=0,
-        ),
-        name=name,
-    )(
-        *[got for _ in columns],
-        *[pltpu.with_memory_space_constraint(p, pltpu.HBM) for p in pieces],
-    )
+        functools.partial(far_kernel, n),
+        out_shape=pltpu.HBM((slots, 2 * width + 128), BF16),
+        in_specs=[anywhere] + [HBM_SPEC, anywhere] * 3 + [vmem] * 7,
+        out_specs=HBM_SPEC,
+        scratch_shapes=[pltpu.VMEM((slots, width), BF16), full, full, full]
+        + [pltpu.VMEM((slots, 2 * width + 128), BF16)]
+        + [pltpu.SemaphoreType.DMA((9,))],
+        name="far_rest",
+        **params(4, 32),
+    )(got, *far_pieces, *sums, *fronts)
 
 
 def forward_end_kernel(back_ref, sel_ref, col_ref, input_ref, out_ref):
     cols = col_ref[...]
-    back = back_ref[...]
+    back = back_ref[:, : input_ref.shape[1]]
     mixed = cols[:, 0:1] * tn_dot(sel_ref[0], back)
     mixed = mixed + cols[:, 1:2] * tn_dot(sel_ref[1], back)
     out_ref[...] = (input_ref[...].astype(F32) + mixed).astype(BF16)
@@ -274,8 +389,8 @@
     cols = col_ref[...]
     width = saved_ref.shape[1]
     experts = router_ref.shape[0]
-    back = back_ref[:, :width]
-    tail = back_ref[:, width:]
+    back = back_ref[:, width : 2 * width]
+    tail = back_ref[:, 2 * width :]
     change = [
         cols[:, 4 + k : 5 + k] * tn_dot(sel_ref[k], tail)[:, 0:1] for k in range(2)
     ]
@@ -331,6 +446,10 @@
     return blocks.reshape(rows.shape)
 
 
+def paired(held, passed):
+    return [w for h, p in zip(held, passed) for w in (*in_hbm(h), p)]
+
+
 def on_device(
     section_input,
     saved_input,
@@ -344,33 +463,37 @@
     down_weight,
 ):
     own = (gate_weight[0].T, up_weight[0].T, down_weight[0])
-    far = [lax.ppermute(w, "expert", z_partners()) for w in own]
-    near = [lax.ppermute(w, "expert", core_partners()) for w in own]
-    cross = [lax.ppermute(w, "expert", core_partners()) for w in far]
-    pieces = [w for four in zip(own, near, far, cross) for w in four]
+    across, between = z_partners(), core_partners()
+    far = [lax.ppermute(w, "expert", across) for w in own]
+    near = in_hbm(*[lax.ppermute(w, "expert", between) for w in own])
     ids = expert_ids[0].transpose(0, 2, 1)
     keep = keep_mask[0].transpose(0, 2, 1)
     router_t = router_weight[0].T
-    experts = router_t.shape[0]
-    slots = experts * 16
+    slots = router_t.shape[0] * 16
     send, fsel, fcol, bsel, bcol = prologue(
         section_input[0], saved_input[0], grad_input[0], ids, keep, norm_gain, router_t, slots
     )
+    send, far[0] = lax.optimization_barrier((send, far[0]))
     got = trade(send)
-    out_f = expert_call(forward_kernel, got, (0,), 0, 1, pieces, "forward_rows")
-    back_f = trade(out_f)
-    out_b = expert_call(backward_kernel, got, (1, 2), 128, 2, pieces, "backward_rows")
-    back_b = trade(out_b)
+
+    def cross(pieces, sums):
+        late, sums = lax.optimization_barrier((pieces[1:], sums))
+        pieces = [pieces[0], *late]
+        crossed = [lax.ppermute(w, "expert", between) for w in pieces]
+        return paired(pieces, crossed), sums
+
+    out = expert_calls(got, paired(own, near), far, cross)
+    back = trade(out)
     mixed = end_call(
-        forward_end_kernel, (back_f, fsel, fcol, section_input[0]), section_input[0], "forward_end"
+        forward_end_kernel, (back, fsel, fcol, section_input[0]), section_input[0], "forward_end"
     )
     input_grad = end_call(
         backward_end_kernel,
-        (back_b, bsel, bcol, saved_input[0], grad_input[0], norm_gain, router_t),
+        (back, bsel, bcol, saved_input[0], grad_input[0], norm_gain, router_t),
         saved_input[0],
         "backward_end",
     )
-    return (shifted(mixed, 1)[None], shifted(input_grad, -1)[None])
+    return (shifted(mixed[None], 1), shifted(input_grad[None], -1))
 
 
 def solution(mesh):

time: 235 us -> 222 us (0.945)
  blocking collectives: 0 us -> 64.8 us
  waiting for transfers between devices: 126 us -> 82.1 us
  starting transfers between devices: 70 us -> 49.4 us
  local copies, waits for them, and re-layouts: 17.6 us -> 2.47 us
  Pallas kernels: 19.5 us -> 22.1 us
    all_to_all x0 -> x1, blocking collectives: none -> 64.8 us  [trade(): lax.all_to_all(blocks, 'expert', 0, 0, axis_index_groups=groups, tiled=True)]
    ppermute x9, waiting for transfers between devices: 72.5 us -> 11 us  [the longest x3 10.9 us: on_device(): far = [lax.ppermute(w, 'expert', across) for w in own]]
    unnamed x64 -> x16, local copies, waits for them, and re-layouts: 17.6 us -> 2.47 us
    all_to_all x3 -> x1, waiting for transfers between devices: 45.6 us -> 60.4 us  [trade(): lax.all_to_all(blocks, 'expert', 0, 0, axis_index_groups=groups, tiled=True)]
    all_to_all x3 -> x1, starting transfers between devices: 28.3 us -> 15.8 us  [trade(): lax.all_to_all(blocks, 'expert', 0, 0, axis_index_groups=groups, tiled=True)]
    ppermute x9, starting transfers between devices: 33.5 us -> 26.7 us  [the longest x3 10.1 us: on_device(): far = [lax.ppermute(w, 'expert', across) for w in own]]
    pallas_call x3 -> x4, Pallas kernels: 16.1 us -> 20 us  [the longest x1 6.96 us: expert_calls(): pl.pallas_call(functools.partial(near_kernel, n), out_shape=[shape(width,...]
    ppermute x2, waiting for transfers between devices: 7.97 us -> 10.7 us  [shifted(): lax.ppermute(block, 'section', [((i - distance) % n, i) for i in range(n)])]
  transfers between devices with their start and end apart: 14 -> 12, of which waited for: 6 -> 6; matrix products, arithmetic and copies ran while one was open for 0% -> 0% of each run, Pallas kernels for 5% -> 7%
where the time goes in v1:
time: 222 us
  waiting for transfers between devices  82.1 us (37%)
  blocking collectives  64.8 us (29%)
  starting transfers between devices  49.4 us (22%)
  Pallas kernels  22.1 us (10%)
  local copies, waits for them, and re-layouts  2.47 us (1%)
    all_to_all x1, blocking collectives, trade(): lax.all_to_all(blocks, 'expert', 0, 0, axis_index_groups=groups, tiled=True)  64.8 us
    all_to_all x1, waiting for transfers between devices, trade(): lax.all_to_all(blocks, 'expert', 0, 0, axis_index_groups=groups, tiled=True)  60.4 us
    all_to_all x1, starting transfers between devices, trade(): lax.all_to_all(blocks, 'expert', 0, 0, axis_index_groups=groups, tiled=True)  15.8 us
    ppermute x3, waiting for transfers between devices, on_device(): far = [lax.ppermute(w, 'expert', across) for w in own]  10.9 us
    ppermute x2, waiting for transfers between devices, shifted(): lax.ppermute(block, 'section', [((i - distance) % n, i) for i in range(n)])  10.7 us
    ppermute x3, starting transfers between devices, on_device(): far = [lax.ppermute(w, 'expert', across) for w in own]  10.1 us
    ppermute x3, starting transfers between devices, cross(): crossed = [lax.ppermute(w, 'expert', between) for w in pieces]  8.48 us
    ppermute x3, starting transfers between devices, on_device(): near = in_hbm(*[lax.ppermute(w, 'expert', between) for w in own])  8.07 us
  transfers between devices with their start and end apart: 12, of which 6 were waited for; matrix products, arithmetic and copies ran while one was open for 0% of the time, Pallas kernels for 7%

profile of v1, /device:TPU:1, one launch (start us, length us, event | category | flops | bytes accessed | tf_op | source)
XLA Modules:
  0.0 221.8 jit_solution(10634288209886922485)
XLA Ops:
  0.6 4.8 %collective-permute-start = (bf16[192,2048]{1,0:T(8,128)(2,1)}, bf16[192,2048]{1,0:T(8,128)(2,1)}, u32[]{:S(2)}, u32[]{:S(2)}) collective-permute-start(bf16[192,2048]{1,0:T(8,128)(2,1)} %bitcast.44), channel_id=1, source_target_pairs={{0,2},{1,3},{2,0},{3,1},{4,6},{5,7},{6,4},{7,5},{8,10},{9,11},{10,... | collective-permute-start | bytes 2359304 | tf_op jit(solution)/shard_map/ppermute | solution.py:467
  5.5 4.0 %prologue.1 = (bf16[256,6144]{1,0:T(8,128)(2,1)}, bf16[2,256,96]{2,1,0:T(8,128)(2,1)S(1)}, f32[96,128]{1,0:T(8,128)S(1)}, bf16[2,256,96]{2,1,0:T(8,128)(2,1)S(1)}, f32[96,128]{1,0:T(8,128)S(1)}) custom-call(bf16[96,2048]{1,0:T(8,128)(2,1)} %bitcast.34, bf16[96,2048]{1,0:T(8,128)(2,1)} %bitcast.30, bf16[96,2048]{1,0:T(8,128)(2,1)} %bitcast.32, ...), custom_call_target="tpu_custom_call" | custom-call | flops 301989888 | bytes 5242880 | tf_op jit(solution)/shard_map/prologue/pallas_call | solution.py:187
  9.5 9.4 %collective-permute-done.refs_1_ = bf16[192,2048]{1,0:T(8,128)(2,1)} collective-permute-done((bf16[192,2048]{1,0:T(8,128)(2,1)}, bf16[192,2048]{1,0:T(8,128)(2,1)}, u32[]{:S(2)}, u32[]{:S(2)}) %collective-permute-start) | collective-permute-done | bytes 786464 | tf_op jit(solution)/shard_map/ppermute | solution.py:467
  18.9 15.8 %all-to-all-start = ((bf16[16,16,6144]{2,1,0:T(8,128)(2,1)}), bf16[16,16,6144]{2,1,0:T(8,128)(2,1)S(1)}, u32[]{:S(2)}, u32[]{:S(2)}) async-start(bf16[16,16,6144]{2,1,0:T(8,128)(2,1)} %bitcast.41), calls=%async_computation | async-start | bytes 6291456 | tf_op jit(solution)/shard_map/all_to_all | solution.py:443
  34.7 3.7 %collective-permute-start.4 = (bf16[192,2048]{1,0:T(8,128)(2,1)}, bf16[192,2048]{1,0:T(8,128)(2,1)S(1)}, u32[]{:S(2)}, u32[]{:S(2)}) collective-permute-start(bf16[192,2048]{1,0:T(8,128)(2,1)} %bitcast.45), channel_id=1, source_target_pairs={{0,1},{1,0},{2,3},{3,2},{4,5},{5,4},{6,7},{7,6},{8,9},{9,8},{10,11... | collective-permute-start | bytes 2359304 | tf_op jit(solution)/shard_map/ppermute | solution.py:468
  38.4 1.9 collective-permute-start.5
  40.4 2.4 %collective-permute-start.6 = (bf16[192,2048]{1,0:T(8,128)(2,1)}, bf16[192,2048]{1,0:T(8,128)(2,1)}, u32[]{:S(2)}, u32[]{:S(2)}) collective-permute-start(bf16[192,2048]{1,0:T(8,128)(2,1)} %bitcast.50), channel_id=1, source_target_pairs={{0,1},{1,0},{2,3},{3,2},{4,5},{5,4},{6,7},{7,6},{8,9},{9,8},{10,11... | collective-permute-start | bytes 2359304 | tf_op jit(solution)/shard_map/ppermute | solution.py:468
  42.8 3.1 %collective-permute-start.2 = (bf16[192,2048]{1,0:T(8,128)(2,1)}, bf16[192,2048]{1,0:T(8,128)(2,1)}, u32[]{:S(2)}, u32[]{:S(2)}) collective-permute-start(bf16[192,2048]{1,0:T(8,128)(2,1)} %bitcast.48), channel_id=1, source_target_pairs={{0,2},{1,3},{2,0},{3,1},{4,6},{5,7},{6,4},{7,5},{8,10},{9,11},{10,... | collective-permute-start | bytes 2359304 | tf_op jit(solution)/shard_map/ppermute | solution.py:467
  45.9 2.2 collective-permute-start.3
  48.1 0.0 collective-permute-done.4.refs_2_
  48.1 0.0 copy-start.5
  48.1 2.5 %collective-permute-start.1 = (bf16[192,2048]{1,0:T(8,128)(2,1)}, bf16[192,2048]{1,0:T(8,128)(2,1)}, u32[]{:S(2)}, u32[]{:S(2)}) collective-permute-start(bf16[192,2048]{1,0:T(8,128)(2,1)} %collective-permute-done.refs_1_), channel_id=1, source_target_pairs={{0,1},{1,0},{2,3},{3,2},{4,5},{5,4},{6,7},{7,6},{8,9},{9,8},{10,11... | collective-permute-start | bytes 2359304 | tf_op jit(solution)/shard_map/ppermute | solution.py:482
  50.6 0.0 collective-permute-done.5.refs_4_
  50.6 0.0 copy-done.5
  50.6 0.0 copy-start.6
  50.6 0.9 copy-done.6
  51.6 0.0 collective-permute-done.6.refs_6_
  51.6 60.4 %all-to-all-done = bf16[16,16,6144]{2,1,0:T(8,128)(2,1)S(1)} async-done(((bf16[16,16,6144]{2,1,0:T(8,128)(2,1)}), bf16[16,16,6144]{2,1,0:T(8,128)(2,1)S(1)}, u32[]{:S(2)}, u32[]{:S(2)}) %all-to-all-start) | async-done | bytes 3145760 | tf_op jit(solution)/shard_map/all_to_all | solution.py:443
  112.0 7.0 %near_share.1 = (f32[256,2048]{1,0:T(8,128)S(1)}, f32[256,2048]{1,0:T(8,128)S(1)}, f32[256,128]{1,0:T(8,128)S(1)}) custom-call(bf16[256,6144]{1,0:T(8,128)(2,1)S(1)} %bitcast.25, bf16[192,2048]{1,0:T(8,128)(2,1)} %bitcast.46, bf16[192,2048]{1,0:T(8,128)(2,1)} %copy-done.5, bf16[192,2048]{1,0:T(8,128)(2,1)} %bitcast.49, bf16[192,2048]{1,0:T(8,128)(2,1)} %copy-done.6, ...), custom_call_target="tpu_custom_call" | custom-call | flops 3221225472 | bytes 8388608 | tf_op jit(solution)/shard_map/near_share/pallas_call | solution.py:339
  118.9 0.0 collective-permute-done.2.refs_3_
  119.0 1.5 collective-permute-done.3.refs_5_
  120.4 4.1 %collective-permute-start.7 = (bf16[192,2048]{1,0:T(8,128)(2,1)}, bf16[192,2048]{1,0:T(8,128)(2,1)S(1)}, u32[]{:S(2)}, u32[]{:S(2)}) collective-permute-start(bf16[192,2048]{1,0:T(8,128)(2,1)} %collective-permute-done.2.refs_3_), channel_id=1, source_target_pairs={{0,1},{1,0},{2,3},{3,2},{4,5},{5,4},{6,7},{7,6},{8,9},{9,8},{10,11... | collective-permute-start | bytes 2359304 | tf_op jit(solution)/shard_map/ppermute | solution.py:482
  124.5 1.9 collective-permute-start.8
  126.4 0.0 collective-permute-done.1.refs_2_
  126.5 0.2 collective-permute-done.7.refs_4_
  126.6 4.1 %far_front.1 = (bf16[256,384]{1,0:T(8,128)(2,1)S(1)}, bf16[256,384]{1,0:T(8,128)(2,1)S(1)}, f32[256,384]{1,0:T(8,128)S(1)}, f32[256,384]{1,0:T(8,128)S(1)}) custom-call(bf16[256,6144]{1,0:T(8,128)(2,1)S(1)} %bitcast.26, bf16[192,2048]{1,0:T(8,128)(2,1)} %collective-permute-done.refs_1_, bf16[192,2048]{1,0:T(8,128)(2,1)} %collective-permute-done.1.refs_2_, ...), custom_call_target="tpu_custom_call" | custom-call | flops 1610612736 | bytes 8388608 | tf_op jit(solution)/shard_map/far_front/pallas_call | solution.py:350
  130.8 0.0 collective-permute-done.8.refs_6_
  130.8 4.8 %far_rest.1 = bf16[256,4224]{1,0:T(8,128)(2,1)} custom-call(bf16[256,6144]{1,0:T(8,128)(2,1)S(1)} %bitcast.27, bf16[192,2048]{1,0:T(8,128)(2,1)} %collective-permute-done.refs_1_, bf16[192,2048]{1,0:T(8,128)(2,1)} %collective-permute-done.1.refs_2_, bf16[192,2048]{1,0:T(8,128)(2,1)} %collective-permute-done.2.refs_3_, ...), custom_call_target="tpu_custom_call" | custom-call | flops 1610612736 | bytes 8388608 | tf_op jit(solution)/shard_map/far_rest/pallas_call | solution.py:365
  135.6 0.0 copy-start
  135.6 0.0 copy-start.1
  135.6 0.0 copy-start.3
  135.6 0.0 copy-start.4
  135.6 64.8 %all_to_all.10 = bf16[16,16,4224]{2,1,0:T(8,128)(2,1)S(1)} all-to-all(bf16[16,16,4224]{2,1,0:T(8,128)(2,1)} %bitcast.40), channel_id=1, replica_groups={{0,4,10,14,16,20,26,30,32,36,42,46,48,52,58,62},{1,5,11,15,17,21,27,31,..., dimensions={0} | all-to-all | bytes 4325376 | tf_op jit(solution)/shard_map/all_to_all | solution.py:443
  200.4 0.0 copy-start.2
  200.4 0.0 copy-done
  200.4 0.0 copy-done.1
  200.4 0.0 copy-done.3
  200.4 0.0 copy-done.4
  200.4 1.6 backward_end.1
  202.1 5.1 %collective-permute-start.10 = (bf16[1,96,2048]{2,1,0:T(8,128)(2,1)S(1)}, bf16[1,96,2048]{2,1,0:T(8,128)(2,1)S(1)}, u32[]{:S(2)}, u32[]{:S(2)}) collective-permute-start(bf16[1,96,2048]{2,1,0:T(8,128)(2,1)S(1)} %bitcast.36), channel_id=1, source_target_pairs={{64,0},{128,64},{192,128},{256,192},{320,256},{384,320},{448,384},... | collective-permute-start | bytes 1179656 | tf_op jit(solution)/shard_map/ppermute | solution.py:44
  207.2 0.0 copy-done.2
  207.2 0.5 forward_end.1
  207.7 1.9 collective-permute-start.9
  209.6 5.2 %collective-permute-done.10 = bf16[1,96,2048]{2,1,0:T(8,128)(2,1)S(1)} collective-permute-done((bf16[1,96,2048]{2,1,0:T(8,128)(2,1)S(1)}, bf16[1,96,2048]{2,1,0:T(8,128)(2,1)S(1)}, u32[]{:S(2)}, u32[]{:S(2)}) %collective-permute-start.10) | collective-permute-done | bytes 393248 | tf_op jit(solution)/shard_map/ppermute | solution.py:44
  214.8 5.6 %collective-permute-done.9 = bf16[1,96,2048]{2,1,0:T(8,128)(2,1)S(1)} collective-permute-done((bf16[1,96,2048]{2,1,0:T(8,128)(2,1)S(1)}, bf16[1,96,2048]{2,1,0:T(8,128)(2,1)S(1)}, u32[]{:S(2)}, u32[]{:S(2)}) %collective-permute-start.9) | collective-permute-done | bytes 393248 | tf_op jit(solution)/shard_map/ppermute | solution.py:44
  220.3 0.7 copy.14
  221.1 0.7 copy.15
Async XLA Ops:
  0.6 18.3 %collective-permute-start = (bf16[192,2048]{1,0:T(8,128)(2,1)}, bf16[192,2048]{1,0:T(8,128)(2,1)}, u32[]{:S(2)}, u32[]{:S(2)}) collective-permute-start(bf16[192,2048]{1,0:T(8,128)(2,1)} %bitcast.44), channel_id=1, source_target_pairs={{0,2},{1,3},{2,0},{3,1},{4,6},{5,7},{6,4},{7,5},{8,10},{9,11},{10,... | collective-permute-start | bytes 2359304 | tf_op jit(solution)/shard_map/ppermute | solution.py:467
  18.9 93.1 %all-to-all-start = ((bf16[16,16,6144]{2,1,0:T(8,128)(2,1)}), bf16[16,16,6144]{2,1,0:T(8,128)(2,1)S(1)}, u32[]{:S(2)}, u32[]{:S(2)}) async-start(bf16[16,16,6144]{2,1,0:T(8,128)(2,1)} %bitcast.41), calls=%async_computation | async-start | bytes 6291456 | tf_op jit(solution)/shard_map/all_to_all | solution.py:443
  34.7 13.4 %collective-permute-start.4 = (bf16[192,2048]{1,0:T(8,128)(2,1)}, bf16[192,2048]{1,0:T(8,128)(2,1)S(1)}, u32[]{:S(2)}, u32[]{:S(2)}) collective-permute-start(bf16[192,2048]{1,0:T(8,128)(2,1)} %bitcast.45), channel_id=1, source_target_pairs={{0,1},{1,0},{2,3},{3,2},{4,5},{5,4},{6,7},{7,6},{8,9},{9,8},{10,11... | collective-permute-start | bytes 2359304 | tf_op jit(solution)/shard_map/ppermute | solution.py:468
  38.4 12.2 %collective-permute-start.5 = (bf16[192,2048]{1,0:T(8,128)(2,1)}, bf16[192,2048]{1,0:T(8,128)(2,1)S(1)}, u32[]{:S(2)}, u32[]{:S(2)}) collective-permute-start(bf16[192,2048]{1,0:T(8,128)(2,1)} %bitcast.47), channel_id=1, source_target_pairs={{0,1},{1,0},{2,3},{3,2},{4,5},{5,4},{6,7},{7,6},{8,9},{9,8},{10,11... | collective-permute-start | bytes 2359304 | tf_op jit(solution)/shard_map/ppermute | solution.py:468
  40.4 11.2 %collective-permute-start.6 = (bf16[192,2048]{1,0:T(8,128)(2,1)}, bf16[192,2048]{1,0:T(8,128)(2,1)}, u32[]{:S(2)}, u32[]{:S(2)}) collective-permute-start(bf16[192,2048]{1,0:T(8,128)(2,1)} %bitcast.50), channel_id=1, source_target_pairs={{0,1},{1,0},{2,3},{3,2},{4,5},{5,4},{6,7},{7,6},{8,9},{9,8},{10,11... | collective-permute-start | bytes 2359304 | tf_op jit(solution)/shard_map/ppermute | solution.py:468
  42.8 76.2 %collective-permute-start.2 = (bf16[192,2048]{1,0:T(8,128)(2,1)}, bf16[192,2048]{1,0:T(8,128)(2,1)}, u32[]{:S(2)}, u32[]{:S(2)}) collective-permute-start(bf16[192,2048]{1,0:T(8,128)(2,1)} %bitcast.48), channel_id=1, source_target_pairs={{0,2},{1,3},{2,0},{3,1},{4,6},{5,7},{6,4},{7,5},{8,10},{9,11},{10,... | collective-permute-start | bytes 2359304 | tf_op jit(solution)/shard_map/ppermute | solution.py:467
  45.9 74.6 %collective-permute-start.3 = (bf16[192,2048]{1,0:T(8,128)(2,1)}, bf16[192,2048]{1,0:T(8,128)(2,1)}, u32[]{:S(2)}, u32[]{:S(2)}) collective-permute-start(bf16[192,2048]{1,0:T(8,128)(2,1)} %bitcast.51), channel_id=1, source_target_pairs={{0,2},{1,3},{2,0},{3,1},{4,6},{5,7},{6,4},{7,5},{8,10},{9,11},{10,... | collective-permute-start | bytes 2359304 | tf_op jit(solution)/shard_map/ppermute | solution.py:467
  48.1 2.5 %copy-start.5 = (bf16[192,2048]{1,0:T(8,128)(2,1)}, bf16[192,2048]{1,0:T(8,128)(2,1)S(1)}, u32[]{:S(2)}) copy-start(bf16[192,2048]{1,0:T(8,128)(2,1)S(1)} %collective-permute-done.4.refs_2_) | copy-start | bytes 2359300
  48.1 78.3 %collective-permute-start.1 = (bf16[192,2048]{1,0:T(8,128)(2,1)}, bf16[192,2048]{1,0:T(8,128)(2,1)}, u32[]{:S(2)}, u32[]{:S(2)}) collective-permute-start(bf16[192,2048]{1,0:T(8,128)(2,1)} %collective-permute-done.refs_1_), channel_id=1, source_target_pairs={{0,1},{1,0},{2,3},{3,2},{4,5},{5,4},{6,7},{7,6},{8,9},{9,8},{10,11... | collective-permute-start | bytes 2359304 | tf_op jit(solution)/shard_map/ppermute | solution.py:482
  50.6 0.9 copy-start.6
  120.4 6.2 %collective-permute-start.7 = (bf16[192,2048]{1,0:T(8,128)(2,1)}, bf16[192,2048]{1,0:T(8,128)(2,1)S(1)}, u32[]{:S(2)}, u32[]{:S(2)}) collective-permute-start(bf16[192,2048]{1,0:T(8,128)(2,1)} %collective-permute-done.2.refs_3_), channel_id=1, source_target_pairs={{0,1},{1,0},{2,3},{3,2},{4,5},{5,4},{6,7},{7,6},{8,9},{9,8},{10,11... | collective-permute-start | bytes 2359304 | tf_op jit(solution)/shard_map/ppermute | solution.py:482
  124.5 6.3 %collective-permute-start.8 = (bf16[192,2048]{1,0:T(8,128)(2,1)}, bf16[192,2048]{1,0:T(8,128)(2,1)S(1)}, u32[]{:S(2)}, u32[]{:S(2)}) collective-permute-start(bf16[192,2048]{1,0:T(8,128)(2,1)} %collective-permute-done.3.refs_5_), channel_id=1, source_target_pairs={{0,1},{1,0},{2,3},{3,2},{4,5},{5,4},{6,7},{7,6},{8,9},{9,8},{10,11... | collective-permute-start | bytes 2359304 | tf_op jit(solution)/shard_map/ppermute | solution.py:482
  135.6 64.8 %copy-start = (bf16[1,96,2048]{2,1,0:T(8,128)(2,1)S(1)}, bf16[1,96,2048]{2,1,0:T(8,128)(2,1)}, u32[]{:S(2)}) copy-start(bf16[1,96,2048]{2,1,0:T(8,128)(2,1)} %param.11) | copy-start | bytes 1179652
  135.6 64.8 %copy-start.1 = (bf16[1,96,2048]{2,1,0:T(8,128)(2,1)S(1)}, bf16[1,96,2048]{2,1,0:T(8,128)(2,1)}, u32[]{:S(2)}) copy-start(bf16[1,96,2048]{2,1,0:T(8,128)(2,1)} %param.12) | copy-start | bytes 1179652
  135.6 64.8 %copy-start.3 = (bf16[1,2048,16]{1,2,0:T(8,128)(2,1)S(1)}, bf16[1,2048,16]{1,2,0:T(8,128)(2,1)}, u32[]{:S(2)}) copy-start(bf16[1,2048,16]{1,2,0:T(8,128)(2,1)} %param.16) | copy-start | bytes 196612
  135.6 64.8 %copy-start.4 = (f32[1,2048]{1,0:T(1,128)S(1)}, f32[1,2048]{1,0:T(1,128)}, u32[]{:S(2)}) copy-start(f32[1,2048]{1,0:T(1,128)} %gain_ref.1) | copy-start | bytes 24580
  200.4 6.7 %copy-start.2 = (bf16[1,96,2048]{2,1,0:T(8,128)(2,1)S(1)}, bf16[1,96,2048]{2,1,0:T(8,128)(2,1)}, u32[]{:S(2)}) copy-start(bf16[1,96,2048]{2,1,0:T(8,128)(2,1)} %param.10) | copy-start | bytes 1179652
  202.1 12.7 %collective-permute-start.10 = (bf16[1,96,2048]{2,1,0:T(8,128)(2,1)S(1)}, bf16[1,96,2048]{2,1,0:T(8,128)(2,1)S(1)}, u32[]{:S(2)}, u32[]{:S(2)}) collective-permute-start(bf16[1,96,2048]{2,1,0:T(8,128)(2,1)S(1)} %bitcast.36), channel_id=1, source_target_pairs={{64,0},{128,64},{192,128},{256,192},{320,256},{384,320},{448,384},... | collective-permute-start | bytes 1179656 | tf_op jit(solution)/shard_map/ppermute | solution.py:44
  207.7 12.6 %collective-permute-start.9 = (bf16[1,96,2048]{2,1,0:T(8,128)(2,1)S(1)}, bf16[1,96,2048]{2,1,0:T(8,128)(2,1)S(1)}, u32[]{:S(2)}, u32[]{:S(2)}) collective-permute-start(bf16[1,96,2048]{2,1,0:T(8,128)(2,1)S(1)} %bitcast.37), channel_id=1, source_target_pairs={{448,0},{0,64},{64,128},{128,192},{192,256},{256,320},{320,384},{3... | collective-permute-start | bytes 1179656 | tf_op jit(solution)/shard_map/ppermute | solution.py:44

commit v2 on v1

--- a/solution.py
+++ b/solution.py
@@ -217,28 +217,41 @@
 STEP = 512
 
 
+def row_loads(got_hbm, rows, batches):
+    slots = got_hbm.shape[0]
+    width = rows.shape[1]
+    return [
+        (got_hbm.at[:, pl.ds(m * width, width)], rows.at[pl.ds(m * slots, slots)])
+        for m in range(batches)
+    ]
+
+
 def near_kernel(n, *refs):
     got_hbm, pieces, refs = refs[0], refs[1 : 1 + 3 * n], refs[1 + 3 * n :]
-    sum_f, sum_b, change_ref, got, gate, up, down, sems = refs
+    sum_f, sum_b, change_ref, rows, gate, up, down, sems = refs
     width = gate.shape[1]
-    pairs = [(got_hbm, got)]
-    pairs += load_pieces(pieces[:n], gate, n)
+    slots = sum_f.shape[0]
+    row_pairs = row_loads(got_hbm, rows, 3)
+    pairs = row_pairs[:2] + load_pieces(pieces[:n], gate, n)
     pairs += load_pieces(pieces[n : 2 * n], up, n)
-    pairs += load_pieces(pieces[2 * n :], down, n)
+    pairs += row_pairs[2:] + load_pieces(pieces[2 * n :], down, n)
     copies = start_copies(pairs, sems)
-    for copy in copies[: 1 + 2 * n]:
-        copy.wait()
-    rows = got[:, :width]
-    act, _, _ = gate_terms(nt_dot(rows, gate[...]), nt_dot(rows, up[...]))
-    for copy in copies[1 + 2 * n :]:
+    for copy in copies[: 2 + n]:
+        copy.wait()
+    both = rows[: 2 * slots, :]
+    pre_gate = nt_dot(both, gate[...])
+    for copy in copies[2 + n : 2 + 2 * n]:
+        copy.wait()
+    pre_up = nt_dot(both, up[...])
+    act, _, _ = gate_terms(pre_gate[:slots], pre_up[:slots])
+    inner, to_gate, to_up = gate_terms(pre_gate[slots:], pre_up[slots:])
+    for copy in copies[2 + 2 * n :]:
         copy.wait()
     for at in range(0, width, STEP):
         sum_f[:, at : at + STEP] = jnp.dot(
             act, down[:, at : at + STEP], preferred_element_type=F32
         )
-    rows = got[:, width : 2 * width]
-    inner, to_gate, to_up = gate_terms(nt_dot(rows, gate[...]), nt_dot(rows, up[...]))
-    pulled = nt_dot(got[:, 2 * width :], down[...])
+    pulled = nt_dot(rows[2 * slots :, :], down[...])
     change = jnp.sum(inner.astype(F32) * pulled, axis=1, keepdims=True)
     change_ref[...] = jnp.broadcast_to(change, change_ref.shape)
     grad_gate = (pulled * to_gate).astype(BF16)
@@ -251,18 +264,20 @@
 
 def front_kernel(n, *refs):
     got_hbm, pieces, refs = refs[0], refs[1 : 1 + 2 * n], refs[1 + 2 * n :]
-    act_ref, inner_ref, to_gate_ref, to_up_ref, got, gate, up, sems = refs
-    width = gate.shape[1]
-    pairs = [(got_hbm.at[:, pl.ds(0, 2 * width)], got)]
-    pairs += load_pieces(pieces[:n], gate, n)
+    act_ref, inner_ref, to_gate_ref, to_up_ref, rows, gate, up, sems = refs
+    slots = act_ref.shape[0]
+    pairs = row_loads(got_hbm, rows, 2) + load_pieces(pieces[:n], gate, n)
     pairs += load_pieces(pieces[n:], up, n)
-    for copy in start_copies(pairs, sems):
-        copy.wait()
-    rows = got[:, :width]
-    act, _, _ = gate_terms(nt_dot(rows, gate[...]), nt_dot(rows, up[...]))
+    copies = start_copies(pairs, sems)
+    for copy in copies[: 2 + n]:
+        copy.wait()
+    pre_gate = nt_dot(rows[...], gate[...])
+    for copy in copies[2 + n :]:
+        copy.wait()
+    pre_up = nt_dot(rows[...], up[...])
+    act, _, _ = gate_terms(pre_gate[:slots], pre_up[:slots])
     act_ref[...] = act
-    rows = got[:, width:]
-    inner, to_gate, to_up = gate_terms(nt_dot(rows, gate[...]), nt_dot(rows, up[...]))
+    inner, to_gate, to_up = gate_terms(pre_gate[slots:], pre_up[slots:])
     inner_ref[...] = inner
     to_gate_ref[...] = to_gate
     to_up_ref[...] = to_up
@@ -341,8 +356,8 @@
         out_shape=[shape(width, F32), shape(width, F32), shape(128, F32)],
         in_specs=[anywhere] + [HBM_SPEC] * 6,
         out_specs=[vmem] * 3,
-        scratch_shapes=[pltpu.VMEM(got.shape, BF16), full, full, full]
-        + [pltpu.SemaphoreType.DMA((7,))],
+        scratch_shapes=[pltpu.VMEM((3 * slots, width), BF16), full, full, full]
+        + [pltpu.SemaphoreType.DMA((9,))],
         name="near_share",
         **params(8, 32),
     )(got, *near_pieces)
@@ -357,8 +372,8 @@
         ],
         in_specs=[anywhere] + [HBM_SPEC, anywhere] * 2,
         out_specs=[vmem] * 4,
-        scratch_shapes=[pltpu.VMEM((slots, 2 * width), BF16), full, full]
-        + [pltpu.SemaphoreType.DMA((5,))],
+        scratch_shapes=[pltpu.VMEM((2 * slots, width), BF16), full, full]
+        + [pltpu.SemaphoreType.DMA((6,))],
         name="far_front",
         **params(4, 24),
     )(got, *far_pieces[:4])
@@ -375,19 +390,17 @@
     )(got, *far_pieces, *sums, *fronts)
 
 
-def forward_end_kernel(back_ref, sel_ref, col_ref, input_ref, out_ref):
+def end_kernel(
+    back_ref, fsel_ref, fcol_ref, sel_ref, col_ref, input_ref, saved_ref, upstream_ref,
+    gain_ref, router_ref, mixed_ref, out_ref,
+):
+    width = saved_ref.shape[1]
+    cols = fcol_ref[...]
+    back = back_ref[:, :width]
+    mixed = cols[:, 0:1] * tn_dot(fsel_ref[0], back)
+    mixed = mixed + cols[:, 1:2] * tn_dot(fsel_ref[1], back)
+    mixed_ref[...] = (input_ref[...].astype(F32) + mixed).astype(BF16)
     cols = col_ref[...]
-    back = back_ref[:, : input_ref.shape[1]]
-    mixed = cols[:, 0:1] * tn_dot(sel_ref[0], back)
-    mixed = mixed + cols[:, 1:2] * tn_dot(sel_ref[1], back)
-    out_ref[...] = (input_ref[...].astype(F32) + mixed).astype(BF16)
-
-
-def backward_end_kernel(
-    back_ref, sel_ref, col_ref, saved_ref, upstream_ref, gain_ref, router_ref, out_ref
-):
-    cols = col_ref[...]
-    width = saved_ref.shape[1]
     experts = router_ref.shape[0]
     back = back_ref[:, width : 2 * width]
     tail = back_ref[:, 2 * width :]
@@ -419,20 +432,21 @@
     out_ref[...] = (upstream_ref[...].astype(F32) + norm_grad).astype(BF16)
 
 
-def end_call(kernel, args, like, name):
+def end_call(*args):
+    like = jax.ShapeDtypeStruct(args[5].shape, BF16)
+    vmem = pl.BlockSpec(memory_space=pltpu.VMEM)
     return pl.pallas_call(
-        kernel,
-        out_shape=jax.ShapeDtypeStruct(like.shape, BF16),
-        grid=(1,),
-        in_specs=[whole(a.shape) for a in args],
-        out_specs=whole(like.shape),
-        compiler_params=pltpu.CompilerParams(vmem_limit_bytes=40 * MIB),
+        end_kernel,
+        out_shape=[like, like],
+        in_specs=[vmem] * len(args),
+        out_specs=[vmem] * 2,
+        compiler_params=pltpu.CompilerParams(vmem_limit_bytes=24 * MIB),
         cost_estimate=pl.CostEstimate(
-            flops=4 * args[0].shape[0] * like.shape[0] * like.shape[1],
-            bytes_accessed=3 * MIB,
+            flops=8 * args[0].shape[0] * like.shape[0] * like.shape[1],
+            bytes_accessed=4 * MIB,
             transcendentals=0,
         ),
-        name=name,
+        name="finish",
     )(*args)
 
 
@@ -465,7 +479,7 @@
     own = (gate_weight[0].T, up_weight[0].T, down_weight[0])
     across, between = z_partners(), core_partners()
     far = [lax.ppermute(w, "expert", across) for w in own]
-    near = in_hbm(*[lax.ppermute(w, "expert", between) for w in own])
+    near = [lax.ppermute(w, "expert", between) for w in own]
     ids = expert_ids[0].transpose(0, 2, 1)
     keep = keep_mask[0].transpose(0, 2, 1)
     router_t = router_weight[0].T
@@ -474,24 +488,19 @@
         section_input[0], saved_input[0], grad_input[0], ids, keep, norm_gain, router_t, slots
     )
     send, far[0] = lax.optimization_barrier((send, far[0]))
+    near = in_hbm(*near)
     got = trade(send)
 
     def cross(pieces, sums):
-        late, sums = lax.optimization_barrier((pieces[1:], sums))
-        pieces = [pieces[0], *late]
+        last, sums = lax.optimization_barrier((pieces[2], sums))
+        pieces = [*pieces[:2], last]
         crossed = [lax.ppermute(w, "expert", between) for w in pieces]
         return paired(pieces, crossed), sums
 
     out = expert_calls(got, paired(own, near), far, cross)
     back = trade(out)
-    mixed = end_call(
-        forward_end_kernel, (back, fsel, fcol, section_input[0]), section_input[0], "forward_end"
-    )
-    input_grad = end_call(
-        backward_end_kernel,
-        (back, bsel, bcol, saved_input[0], grad_input[0], norm_gain, router_t),
-        saved_input[0],
-        "backward_end",
+    mixed, input_grad = end_call(
+        back, fsel, fcol, bsel, bcol, section_input[0], saved_input[0], grad_input[0], norm_gain, router_t
     )
     return (shifted(mixed[None], 1), shifted(input_grad[None], -1))
 

time: 222 us -> 220 us (level)
  waiting for transfers between devices: 82.1 us -> 77.6 us
  starting transfers between devices: 49.4 us -> 52 us
    all_to_all x1, waiting for transfers between devices: 60.4 us -> 2.62 us  [trade(): lax.all_to_all(blocks, 'expert', 0, 0, axis_index_groups=groups, tiled=True)]
    ppermute x3, waiting for transfers between devices: 10.9 us -> 64.2 us  [on_device(): far = [lax.ppermute(w, 'expert', across) for w in own]]
    ppermute x3, starting transfers between devices: 8.48 us -> 10.7 us  [cross(): crossed = [lax.ppermute(w, 'expert', between) for w in pieces]]
where the time goes in v2:
time: 220 us
  waiting for transfers between devices  77.6 us (35%)
  blocking collectives  65.1 us (30%)
  starting transfers between devices  52 us (24%)
  Pallas kernels  21.7 us (10%)
  local copies, waits for them, and re-layouts  2.44 us (1%)
    all_to_all x1, blocking collectives, trade(): lax.all_to_all(blocks, 'expert', 0, 0, axis_index_groups=groups, tiled=True)  65.1 us
    ppermute x3, waiting for transfers between devices, on_device(): far = [lax.ppermute(w, 'expert', across) for w in own]  64.2 us
    all_to_all x1, starting transfers between devices, trade(): lax.all_to_all(blocks, 'expert', 0, 0, axis_index_groups=groups, tiled=True)  15.8 us
    ppermute x2, waiting for transfers between devices, shifted(): lax.ppermute(block, 'section', [((i - distance) % n, i) for i in range(n)])  10.8 us
    ppermute x3, starting transfers between devices, cross(): crossed = [lax.ppermute(w, 'expert', between) for w in pieces]  10.7 us
    ppermute x3, starting transfers between devices, on_device(): far = [lax.ppermute(w, 'expert', across) for w in own]  10.1 us
    ppermute x3, starting transfers between devices, on_device(): near = [lax.ppermute(w, 'expert', between) for w in own]  8.35 us
    ppermute x2, starting transfers between devices, shifted(): lax.ppermute(block, 'section', [((i - distance) % n, i) for i in range(n)])  7.05 us
  transfers between devices with their start and end apart: 12, of which 6 were waited for; matrix products, arithmetic and copies ran while one was open for 0% of the time, Pallas kernels for 7%

profile of v2, /device:TPU:1, one launch (start us, length us, event | category | flops | bytes accessed | tf_op | source)
XLA Modules:
  0.0 219.8 jit_solution(14853326626866773028)
XLA Ops:
  0.6 4.8 %collective-permute-start = (bf16[192,2048]{1,0:T(8,128)(2,1)}, bf16[192,2048]{1,0:T(8,128)(2,1)}, u32[]{:S(2)}, u32[]{:S(2)}) collective-permute-start(bf16[192,2048]{1,0:T(8,128)(2,1)} %bitcast.43), channel_id=1, source_target_pairs={{0,2},{1,3},{2,0},{3,1},{4,6},{5,7},{6,4},{7,5},{8,10},{9,11},{10,... | collective-permute-start | bytes 2359304 | tf_op jit(solution)/shard_map/ppermute | solution.py:481
  5.5 4.0 %prologue.1 = (bf16[256,6144]{1,0:T(8,128)(2,1)}, bf16[2,256,96]{2,1,0:T(8,128)(2,1)S(1)}, f32[96,128]{1,0:T(8,128)S(1)}, bf16[2,256,96]{2,1,0:T(8,128)(2,1)S(1)}, f32[96,128]{1,0:T(8,128)S(1)}) custom-call(bf16[96,2048]{1,0:T(8,128)(2,1)} %bitcast.29, bf16[96,2048]{1,0:T(8,128)(2,1)} %bitcast.31, bf16[96,2048]{1,0:T(8,128)(2,1)} %bitcast.33, ...), custom_call_target="tpu_custom_call" | custom-call | flops 301989888 | bytes 5242880 | tf_op jit(solution)/shard_map/prologue/pallas_call | solution.py:187
  9.5 9.4 %collective-permute-done.refs_1_ = bf16[192,2048]{1,0:T(8,128)(2,1)} collective-permute-done((bf16[192,2048]{1,0:T(8,128)(2,1)}, bf16[192,2048]{1,0:T(8,128)(2,1)}, u32[]{:S(2)}, u32[]{:S(2)}) %collective-permute-start) | collective-permute-done | bytes 786464 | tf_op jit(solution)/shard_map/ppermute | solution.py:481
  18.9 15.8 %all-to-all-start = ((bf16[16,16,6144]{2,1,0:T(8,128)(2,1)}), bf16[16,16,6144]{2,1,0:T(8,128)(2,1)S(1)}, u32[]{:S(2)}, u32[]{:S(2)}) async-start(bf16[16,16,6144]{2,1,0:T(8,128)(2,1)} %bitcast.40), calls=%async_computation | async-start | bytes 6291456 | tf_op jit(solution)/shard_map/all_to_all | solution.py:457
  34.7 3.7 %collective-permute-start.5 = (bf16[192,2048]{1,0:T(8,128)(2,1)}, bf16[192,2048]{1,0:T(8,128)(2,1)S(1)}, u32[]{:S(2)}, u32[]{:S(2)}) collective-permute-start(bf16[192,2048]{1,0:T(8,128)(2,1)} %bitcast.44), channel_id=1, source_target_pairs={{0,1},{1,0},{2,3},{3,2},{4,5},{5,4},{6,7},{7,6},{8,9},{9,8},{10,11... | collective-permute-start | bytes 2359304 | tf_op jit(solution)/shard_map/ppermute | solution.py:482
  38.4 1.9 collective-permute-start.6
  40.4 3.1 %collective-permute-start.2 = (bf16[192,2048]{1,0:T(8,128)(2,1)}, bf16[192,2048]{1,0:T(8,128)(2,1)}, u32[]{:S(2)}, u32[]{:S(2)}) collective-permute-start(bf16[192,2048]{1,0:T(8,128)(2,1)} %bitcast.47), channel_id=1, source_target_pairs={{0,2},{1,3},{2,0},{3,1},{4,6},{5,7},{6,4},{7,5},{8,10},{9,11},{10,... | collective-permute-start | bytes 2359304 | tf_op jit(solution)/shard_map/ppermute | solution.py:481
  43.5 2.7 %collective-permute-start.7 = (bf16[192,2048]{1,0:T(8,128)(2,1)}, bf16[192,2048]{1,0:T(8,128)(2,1)}, u32[]{:S(2)}, u32[]{:S(2)}) collective-permute-start(bf16[192,2048]{1,0:T(8,128)(2,1)} %bitcast.49), channel_id=1, source_target_pairs={{0,1},{1,0},{2,3},{3,2},{4,5},{5,4},{6,7},{7,6},{8,9},{9,8},{10,11... | collective-permute-start | bytes 2359304 | tf_op jit(solution)/shard_map/ppermute | solution.py:482
  46.2 2.2 %collective-permute-start.4 = (bf16[192,2048]{1,0:T(8,128)(2,1)}, bf16[192,2048]{1,0:T(8,128)(2,1)}, u32[]{:S(2)}, u32[]{:S(2)}) collective-permute-start(bf16[192,2048]{1,0:T(8,128)(2,1)} %bitcast.50), channel_id=1, source_target_pairs={{0,2},{1,3},{2,0},{3,1},{4,6},{5,7},{6,4},{7,5},{8,10},{9,11},{10,... | collective-permute-start | bytes 2359304 | tf_op jit(solution)/shard_map/ppermute | solution.py:481
  48.4 0.0 collective-permute-done.5.refs_2_
  48.4 0.0 copy-start.5
  48.4 2.2 %collective-permute-start.1 = (bf16[192,2048]{1,0:T(8,128)(2,1)}, bf16[192,2048]{1,0:T(8,128)(2,1)}, u32[]{:S(2)}, u32[]{:S(2)}) collective-permute-start(bf16[192,2048]{1,0:T(8,128)(2,1)} %collective-permute-done.refs_1_), channel_id=1, source_target_pairs={{0,1},{1,0},{2,3},{3,2},{4,5},{5,4},{6,7},{7,6},{8,9},{9,8},{10,11... | collective-permute-start | bytes 2359304 | tf_op jit(solution)/shard_map/ppermute | solution.py:497
  50.6 53.0 %collective-permute-done.2.refs_3_ = bf16[192,2048]{1,0:T(8,128)(2,1)} collective-permute-done((bf16[192,2048]{1,0:T(8,128)(2,1)}, bf16[192,2048]{1,0:T(8,128)(2,1)}, u32[]{:S(2)}, u32[]{:S(2)}) %collective-permute-start.2) | collective-permute-done | bytes 786464 | tf_op jit(solution)/shard_map/ppermute | solution.py:481
  103.6 4.8 %collective-permute-start.3 = (bf16[192,2048]{1,0:T(8,128)(2,1)}, bf16[192,2048]{1,0:T(8,128)(2,1)}, u32[]{:S(2)}, u32[]{:S(2)}) collective-permute-start(bf16[192,2048]{1,0:T(8,128)(2,1)} %collective-permute-done.2.refs_3_), channel_id=1, source_target_pairs={{0,1},{1,0},{2,3},{3,2},{4,5},{5,4},{6,7},{7,6},{8,9},{9,8},{10,11... | collective-permute-start | bytes 2359304 | tf_op jit(solution)/shard_map/ppermute | solution.py:497
  108.4 0.0 collective-permute-done.6.refs_4_
  108.4 0.0 copy-done.5
  108.4 0.0 copy-start.6
  108.4 0.9 copy-done.6
  109.3 0.0 collective-permute-done.7.refs_6_
  109.4 2.6 %all-to-all-done = bf16[16,16,6144]{2,1,0:T(8,128)(2,1)S(1)} async-done(((bf16[16,16,6144]{2,1,0:T(8,128)(2,1)}), bf16[16,16,6144]{2,1,0:T(8,128)(2,1)S(1)}, u32[]{:S(2)}, u32[]{:S(2)}) %all-to-all-start) | async-done | bytes 3145760 | tf_op jit(solution)/shard_map/all_to_all | solution.py:457
  112.0 6.6 %near_share.1 = (f32[256,2048]{1,0:T(8,128)S(1)}, f32[256,2048]{1,0:T(8,128)S(1)}, f32[256,128]{1,0:T(8,128)S(1)}) custom-call(bf16[256,6144]{1,0:T(8,128)(2,1)S(1)} %bitcast.25, bf16[192,2048]{1,0:T(8,128)(2,1)} %bitcast.45, bf16[192,2048]{1,0:T(8,128)(2,1)} %copy-done.5, bf16[192,2048]{1,0:T(8,128)(2,1)} %bitcast.48, bf16[192,2048]{1,0:T(8,128)(2,1)} %copy-done.6, ...), custom_call_target="tpu_custom_call" | custom-call | flops 3221225472 | bytes 8388608 | tf_op jit(solution)/shard_map/near_share/pallas_call | solution.py:354
  118.6 1.8 collective-permute-done.4.refs_5_
  120.4 3.7 %collective-permute-start.8 = (bf16[192,2048]{1,0:T(8,128)(2,1)}, bf16[192,2048]{1,0:T(8,128)(2,1)S(1)}, u32[]{:S(2)}, u32[]{:S(2)}) collective-permute-start(bf16[192,2048]{1,0:T(8,128)(2,1)} %collective-permute-done.4.refs_5_), channel_id=1, source_target_pairs={{0,1},{1,0},{2,3},{3,2},{4,5},{5,4},{6,7},{7,6},{8,9},{9,8},{10,11... | collective-permute-start | bytes 2359304 | tf_op jit(solution)/shard_map/ppermute | solution.py:497
  124.1 0.0 collective-permute-done.3.refs_4_
  124.1 0.0 collective-permute-done.1.refs_2_
  124.2 4.1 %far_front.1 = (bf16[256,384]{1,0:T(8,128)(2,1)S(1)}, bf16[256,384]{1,0:T(8,128)(2,1)S(1)}, f32[256,384]{1,0:T(8,128)S(1)}, f32[256,384]{1,0:T(8,128)S(1)}) custom-call(bf16[256,6144]{1,0:T(8,128)(2,1)S(1)} %bitcast.26, bf16[192,2048]{1,0:T(8,128)(2,1)} %collective-permute-done.refs_1_, bf16[192,2048]{1,0:T(8,128)(2,1)} %collective-permute-done.1.refs_2_, ...), custom_call_target="tpu_custom_call" | custom-call | flops 1610612736 | bytes 8388608 | tf_op jit(solution)/shard_map/far_front/pallas_call | solution.py:365
  128.3 0.0 collective-permute-done.8.refs_6_
  128.3 4.8 %far_rest.1 = bf16[256,4224]{1,0:T(8,128)(2,1)} custom-call(bf16[256,6144]{1,0:T(8,128)(2,1)S(1)} %bitcast.27, bf16[192,2048]{1,0:T(8,128)(2,1)} %collective-permute-done.refs_1_, bf16[192,2048]{1,0:T(8,128)(2,1)} %collective-permute-done.1.refs_2_, bf16[192,2048]{1,0:T(8,128)(2,1)} %collective-permute-done.2.refs_3_, ...), custom_call_target="tpu_custom_call" | custom-call | flops 1610612736 | bytes 8388608 | tf_op jit(solution)/shard_map/far_rest/pallas_call | solution.py:380
  133.2 0.0 copy-start
  133.2 0.0 copy-start.1
  133.2 0.0 copy-start.2
  133.2 0.0 copy-start.3
  133.2 0.0 copy-start.4
  133.2 65.1 %all_to_all.10 = bf16[16,16,4224]{2,1,0:T(8,128)(2,1)S(1)} all-to-all(bf16[16,16,4224]{2,1,0:T(8,128)(2,1)} %bitcast.39), channel_id=1, replica_groups={{0,4,10,14,16,20,26,30,32,36,42,46,48,52,58,62},{1,5,11,15,17,21,27,31,..., dimensions={0} | all-to-all | bytes 4325376 | tf_op jit(solution)/shard_map/all_to_all | solution.py:457
  198.3 0.0 copy-done
  198.3 0.0 copy-done.1
  198.3 0.0 copy-done.2
  198.3 0.0 copy-done.3
  198.3 0.0 copy-done.4
  198.3 2.1 finish.1
  200.5 5.1 %collective-permute-start.10 = (bf16[1,96,2048]{2,1,0:T(8,128)(2,1)S(1)}, bf16[1,96,2048]{2,1,0:T(8,128)(2,1)S(1)}, u32[]{:S(2)}, u32[]{:S(2)}) collective-permute-start(bf16[1,96,2048]{2,1,0:T(8,128)(2,1)S(1)} %bitcast.38), channel_id=1, source_target_pairs={{64,0},{128,64},{192,128},{256,192},{320,256},{384,320},{448,384},... | collective-permute-start | bytes 1179656 | tf_op jit(solution)/shard_map/ppermute | solution.py:44
  205.6 1.9 collective-permute-start.9
  207.5 5.7 %collective-permute-done.10 = bf16[1,96,2048]{2,1,0:T(8,128)(2,1)S(1)} collective-permute-done((bf16[1,96,2048]{2,1,0:T(8,128)(2,1)S(1)}, bf16[1,96,2048]{2,1,0:T(8,128)(2,1)S(1)}, u32[]{:S(2)}, u32[]{:S(2)}) %collective-permute-start.10) | collective-permute-done | bytes 393248 | tf_op jit(solution)/shard_map/ppermute | solution.py:44
  213.3 5.0 %collective-permute-done.9 = bf16[1,96,2048]{2,1,0:T(8,128)(2,1)S(1)} collective-permute-done((bf16[1,96,2048]{2,1,0:T(8,128)(2,1)S(1)}, bf16[1,96,2048]{2,1,0:T(8,128)(2,1)S(1)}, u32[]{:S(2)}, u32[]{:S(2)}) %collective-permute-start.9) | collective-permute-done | bytes 393248 | tf_op jit(solution)/shard_map/ppermute | solution.py:44
  218.3 0.7 copy.14
  219.0 0.7 copy.15
Async XLA Ops:
  0.6 18.3 %collective-permute-start = (bf16[192,2048]{1,0:T(8,128)(2,1)}, bf16[192,2048]{1,0:T(8,128)(2,1)}, u32[]{:S(2)}, u32[]{:S(2)}) collective-permute-start(bf16[192,2048]{1,0:T(8,128)(2,1)} %bitcast.43), channel_id=1, source_target_pairs={{0,2},{1,3},{2,0},{3,1},{4,6},{5,7},{6,4},{7,5},{8,10},{9,11},{10,... | collective-permute-start | bytes 2359304 | tf_op jit(solution)/shard_map/ppermute | solution.py:481
  18.9 93.1 %all-to-all-start = ((bf16[16,16,6144]{2,1,0:T(8,128)(2,1)}), bf16[16,16,6144]{2,1,0:T(8,128)(2,1)S(1)}, u32[]{:S(2)}, u32[]{:S(2)}) async-start(bf16[16,16,6144]{2,1,0:T(8,128)(2,1)} %bitcast.40), calls=%async_computation | async-start | bytes 6291456 | tf_op jit(solution)/shard_map/all_to_all | solution.py:457
  34.7 13.7 %collective-permute-start.5 = (bf16[192,2048]{1,0:T(8,128)(2,1)}, bf16[192,2048]{1,0:T(8,128)(2,1)S(1)}, u32[]{:S(2)}, u32[]{:S(2)}) collective-permute-start(bf16[192,2048]{1,0:T(8,128)(2,1)} %bitcast.44), channel_id=1, source_target_pairs={{0,1},{1,0},{2,3},{3,2},{4,5},{5,4},{6,7},{7,6},{8,9},{9,8},{10,11... | collective-permute-start | bytes 2359304 | tf_op jit(solution)/shard_map/ppermute | solution.py:482
  38.4 70.0 %collective-permute-start.6 = (bf16[192,2048]{1,0:T(8,128)(2,1)}, bf16[192,2048]{1,0:T(8,128)(2,1)S(1)}, u32[]{:S(2)}, u32[]{:S(2)}) collective-permute-start(bf16[192,2048]{1,0:T(8,128)(2,1)} %bitcast.46), channel_id=1, source_target_pairs={{0,1},{1,0},{2,3},{3,2},{4,5},{5,4},{6,7},{7,6},{8,9},{9,8},{10,11... | collective-permute-start | bytes 2359304 | tf_op jit(solution)/shard_map/ppermute | solution.py:482
  40.4 63.2 %collective-permute-start.2 = (bf16[192,2048]{1,0:T(8,128)(2,1)}, bf16[192,2048]{1,0:T(8,128)(2,1)}, u32[]{:S(2)}, u32[]{:S(2)}) collective-permute-start(bf16[192,2048]{1,0:T(8,128)(2,1)} %bitcast.47), channel_id=1, source_target_pairs={{0,2},{1,3},{2,0},{3,1},{4,6},{5,7},{6,4},{7,5},{8,10},{9,11},{10,... | collective-permute-start | bytes 2359304 | tf_op jit(solution)/shard_map/ppermute | solution.py:481
  43.5 65.9 %collective-permute-start.7 = (bf16[192,2048]{1,0:T(8,128)(2,1)}, bf16[192,2048]{1,0:T(8,128)(2,1)}, u32[]{:S(2)}, u32[]{:S(2)}) collective-permute-start(bf16[192,2048]{1,0:T(8,128)(2,1)} %bitcast.49), channel_id=1, source_target_pairs={{0,1},{1,0},{2,3},{3,2},{4,5},{5,4},{6,7},{7,6},{8,9},{9,8},{10,11... | collective-permute-start | bytes 2359304 | tf_op jit(solution)/shard_map/ppermute | solution.py:482
  46.2 74.3 %collective-permute-start.4 = (bf16[192,2048]{1,0:T(8,128)(2,1)}, bf16[192,2048]{1,0:T(8,128)(2,1)}, u32[]{:S(2)}, u32[]{:S(2)}) collective-permute-start(bf16[192,2048]{1,0:T(8,128)(2,1)} %bitcast.50), channel_id=1, source_target_pairs={{0,2},{1,3},{2,0},{3,1},{4,6},{5,7},{6,4},{7,5},{8,10},{9,11},{10,... | collective-permute-start | bytes 2359304 | tf_op jit(solution)/shard_map/ppermute | solution.py:481
  48.4 60.0 %copy-start.5 = (bf16[192,2048]{1,0:T(8,128)(2,1)}, bf16[192,2048]{1,0:T(8,128)(2,1)S(1)}, u32[]{:S(2)}) copy-start(bf16[192,2048]{1,0:T(8,128)(2,1)S(1)} %collective-permute-done.5.refs_2_) | copy-start | bytes 2359300
  48.4 75.8 %collective-permute-start.1 = (bf16[192,2048]{1,0:T(8,128)(2,1)}, bf16[192,2048]{1,0:T(8,128)(2,1)}, u32[]{:S(2)}, u32[]{:S(2)}) collective-permute-start(bf16[192,2048]{1,0:T(8,128)(2,1)} %collective-permute-done.refs_1_), channel_id=1, source_target_pairs={{0,1},{1,0},{2,3},{3,2},{4,5},{5,4},{6,7},{7,6},{8,9},{9,8},{10,11... | collective-permute-start | bytes 2359304 | tf_op jit(solution)/shard_map/ppermute | solution.py:497
  103.6 20.6 %collective-permute-start.3 = (bf16[192,2048]{1,0:T(8,128)(2,1)}, bf16[192,2048]{1,0:T(8,128)(2,1)}, u32[]{:S(2)}, u32[]{:S(2)}) collective-permute-start(bf16[192,2048]{1,0:T(8,128)(2,1)} %collective-permute-done.2.refs_3_), channel_id=1, source_target_pairs={{0,1},{1,0},{2,3},{3,2},{4,5},{5,4},{6,7},{7,6},{8,9},{9,8},{10,11... | collective-permute-start | bytes 2359304 | tf_op jit(solution)/shard_map/ppermute | solution.py:497
  108.4 0.9 copy-start.6
  120.4 7.9 %collective-permute-start.8 = (bf16[192,2048]{1,0:T(8,128)(2,1)}, bf16[192,2048]{1,0:T(8,128)(2,1)S(1)}, u32[]{:S(2)}, u32[]{:S(2)}) collective-permute-start(bf16[192,2048]{1,0:T(8,128)(2,1)} %collective-permute-done.4.refs_5_), channel_id=1, source_target_pairs={{0,1},{1,0},{2,3},{3,2},{4,5},{5,4},{6,7},{7,6},{8,9},{9,8},{10,11... | collective-permute-start | bytes 2359304 | tf_op jit(solution)/shard_map/ppermute | solution.py:497
  133.2 65.2 %copy-start = (bf16[1,96,2048]{2,1,0:T(8,128)(2,1)S(1)}, bf16[1,96,2048]{2,1,0:T(8,128)(2,1)}, u32[]{:S(2)}) copy-start(bf16[1,96,2048]{2,1,0:T(8,128)(2,1)} %param.10) | copy-start | bytes 1179652
  133.2 65.1 %copy-start.1 = (bf16[1,96,2048]{2,1,0:T(8,128)(2,1)S(1)}, bf16[1,96,2048]{2,1,0:T(8,128)(2,1)}, u32[]{:S(2)}) copy-start(bf16[1,96,2048]{2,1,0:T(8,128)(2,1)} %param.11) | copy-start | bytes 1179652
  133.2 65.1 %copy-start.2 = (bf16[1,96,2048]{2,1,0:T(8,128)(2,1)S(1)}, bf16[1,96,2048]{2,1,0:T(8,128)(2,1)}, u32[]{:S(2)}) copy-start(bf16[1,96,2048]{2,1,0:T(8,128)(2,1)} %param.12) | copy-start | bytes 1179652
  133.2 65.1 %copy-start.3 = (bf16[1,2048,16]{1,2,0:T(8,128)(2,1)S(1)}, bf16[1,2048,16]{1,2,0:T(8,128)(2,1)}, u32[]{:S(2)}) copy-start(bf16[1,2048,16]{1,2,0:T(8,128)(2,1)} %param.16) | copy-start | bytes 196612
  133.2 65.1 %copy-start.4 = (f32[1,2048]{1,0:T(1,128)S(1)}, f32[1,2048]{1,0:T(1,128)}, u32[]{:S(2)}) copy-start(f32[1,2048]{1,0:T(1,128)} %gain_ref.1) | copy-start | bytes 24580
  200.5 12.8 %collective-permute-start.10 = (bf16[1,96,2048]{2,1,0:T(8,128)(2,1)S(1)}, bf16[1,96,2048]{2,1,0:T(8,128)(2,1)S(1)}, u32[]{:S(2)}, u32[]{:S(2)}) collective-permute-start(bf16[1,96,2048]{2,1,0:T(8,128)(2,1)S(1)} %bitcast.38), channel_id=1, source_target_pairs={{64,0},{128,64},{192,128},{256,192},{320,256},{384,320},{448,384},... | collective-permute-start | bytes 1179656 | tf_op jit(solution)/shard_map/ppermute | solution.py:44
  205.6 12.7 %collective-permute-start.9 = (bf16[1,96,2048]{2,1,0:T(8,128)(2,1)S(1)}, bf16[1,96,2048]{2,1,0:T(8,128)(2,1)S(1)}, u32[]{:S(2)}, u32[]{:S(2)}) collective-permute-start(bf16[1,96,2048]{2,1,0:T(8,128)(2,1)S(1)} %bitcast.37), channel_id=1, source_target_pairs={{448,0},{0,64},{64,128},{128,192},{192,256},{256,320},{320,384},{3... | collective-permute-start | bytes 1179656 | tf_op jit(solution)/shard_map/ppermute | solution.py:44

commit v3 on v2

--- a/solution.py
+++ b/solution.py
@@ -158,11 +158,15 @@
     keep = [[keep_ref[m, k : k + 1, :] for k in range(2)] for m in range(2)]
     stores = []
 
+    experts, per = send_ref.shape[1:3]
+
     def put(place, sel, values):
-        part = pl.ds(place * width, width)
-        send_ref[:, part] = jnp.dot(sel, values, preferred_element_type=F32).astype(BF16)
+        rows = jnp.dot(sel, values, preferred_element_type=F32).astype(BF16)
+        send_ref[place] = rows.reshape(experts, per, width)
         store = pltpu.make_async_copy(
-            send_ref.at[:, part], send_hbm.at[:, part], sems.at[7 + place]
+            send_ref.at[place],
+            send_hbm.at[:, pl.ds(place * per, per), :],
+            sems.at[7 + place],
         )
         store.start()
         stores.append(store)
@@ -180,17 +184,22 @@
 
 def prologue(fwd, bwd, upstream, ids, keep, gain, router_t, slots):
     tokens, width = fwd.shape
+    experts = router_t.shape[0]
+    per = slots // experts
     sel = jax.ShapeDtypeStruct((2, slots, tokens), BF16)
     col = jax.ShapeDtypeStruct((tokens, 128), F32)
     vmem = pl.BlockSpec(memory_space=pltpu.VMEM)
     args = (fwd, bwd, upstream, ids, keep, gain, router_t)
     return pl.pallas_call(
         prologue_kernel,
-        out_shape=(pltpu.HBM((slots, 3 * width), BF16), sel, col, sel, col),
+        out_shape=(pltpu.HBM((experts, 3 * per, width), BF16), sel, col, sel, col),
         in_specs=[HBM_SPEC] * len(args),
         out_specs=[HBM_SPEC] + [vmem] * 4,
         scratch_shapes=[pltpu.VMEM(a.shape, a.dtype) for a in args]
-        + [pltpu.VMEM((slots, 3 * width), BF16), pltpu.SemaphoreType.DMA((10,))],
+        + [
+            pltpu.VMEM((3, experts, per, width), BF16),
+            pltpu.SemaphoreType.DMA((10,)),
+        ],
         compiler_params=pltpu.CompilerParams(vmem_limit_bytes=24 * MIB),
         cost_estimate=pl.CostEstimate(
             flops=6 * slots * tokens * width, bytes_accessed=5 * MIB, transcendentals=0
@@ -217,41 +226,49 @@
 STEP = 512
 
 
-def row_loads(got_hbm, rows, batches):
-    slots = got_hbm.shape[0]
-    width = rows.shape[1]
-    return [
-        (got_hbm.at[:, pl.ds(m * width, width)], rows.at[pl.ds(m * slots, slots)])
-        for m in range(batches)
-    ]
+def both_rows(got):
+    sources, rows, width = got.shape
+    return got[:, : rows * 2 // 3, :].reshape(sources * rows * 2 // 3, width)
+
+
+def gradient_rows(got):
+    sources, rows, width = got.shape
+    return got[:, rows * 2 // 3 :, :].reshape(sources * rows // 3, width)
+
+
+def of_batch(values, m, sources):
+    per = values.shape[0] // sources // 2
+    split = values.reshape(sources, 2 * per, values.shape[1])
+    return split[:, m * per : (m + 1) * per].reshape(sources * per, values.shape[1])
 
 
 def near_kernel(n, *refs):
-    got_hbm, pieces, refs = refs[0], refs[1 : 1 + 3 * n], refs[1 + 3 * n :]
-    sum_f, sum_b, change_ref, rows, gate, up, down, sems = refs
+    got, pieces, refs = refs[0], refs[1 : 1 + 3 * n], refs[1 + 3 * n :]
+    sum_f, sum_b, change_ref, gate, up, down, sems = refs
     width = gate.shape[1]
-    slots = sum_f.shape[0]
-    row_pairs = row_loads(got_hbm, rows, 3)
-    pairs = row_pairs[:2] + load_pieces(pieces[:n], gate, n)
+    sources = got.shape[0]
+    pairs = load_pieces(pieces[:n], gate, n)
     pairs += load_pieces(pieces[n : 2 * n], up, n)
-    pairs += row_pairs[2:] + load_pieces(pieces[2 * n :], down, n)
+    pairs += load_pieces(pieces[2 * n :], down, n)
     copies = start_copies(pairs, sems)
-    for copy in copies[: 2 + n]:
-        copy.wait()
-    both = rows[: 2 * slots, :]
+    for copy in copies[:n]:
+        copy.wait()
+    both = both_rows(got)
     pre_gate = nt_dot(both, gate[...])
-    for copy in copies[2 + n : 2 + 2 * n]:
+    for copy in copies[n : 2 * n]:
         copy.wait()
     pre_up = nt_dot(both, up[...])
-    act, _, _ = gate_terms(pre_gate[:slots], pre_up[:slots])
-    inner, to_gate, to_up = gate_terms(pre_gate[slots:], pre_up[slots:])
-    for copy in copies[2 + 2 * n :]:
+    act, _, _ = gate_terms(of_batch(pre_gate, 0, sources), of_batch(pre_up, 0, sources))
+    inner, to_gate, to_up = gate_terms(
+        of_batch(pre_gate, 1, sources), of_batch(pre_up, 1, sources)
+    )
+    for copy in copies[2 * n :]:
         copy.wait()
     for at in range(0, width, STEP):
         sum_f[:, at : at + STEP] = jnp.dot(
             act, down[:, at : at + STEP], preferred_element_type=F32
         )
-    pulled = nt_dot(rows[2 * slots :, :], down[...])
+    pulled = nt_dot(gradient_rows(got), down[...])
     change = jnp.sum(inner.astype(F32) * pulled, axis=1, keepdims=True)
     change_ref[...] = jnp.broadcast_to(change, change_ref.shape)
     grad_gate = (pulled * to_gate).astype(BF16)
@@ -263,33 +280,35 @@
 
 
 def front_kernel(n, *refs):
-    got_hbm, pieces, refs = refs[0], refs[1 : 1 + 2 * n], refs[1 + 2 * n :]
-    act_ref, inner_ref, to_gate_ref, to_up_ref, rows, gate, up, sems = refs
-    slots = act_ref.shape[0]
-    pairs = row_loads(got_hbm, rows, 2) + load_pieces(pieces[:n], gate, n)
+    got, pieces, refs = refs[0], refs[1 : 1 + 2 * n], refs[1 + 2 * n :]
+    act_ref, inner_ref, to_gate_ref, to_up_ref, gate, up, sems = refs
+    sources = got.shape[0]
+    both = both_rows(got)
+    pairs = load_pieces(pieces[:n], gate, n)
     pairs += load_pieces(pieces[n:], up, n)
     copies = start_copies(pairs, sems)
-    for copy in copies[: 2 + n]:
-        copy.wait()
-    pre_gate = nt_dot(rows[...], gate[...])
-    for copy in copies[2 + n :]:
-        copy.wait()
-    pre_up = nt_dot(rows[...], up[...])
-    act, _, _ = gate_terms(pre_gate[:slots], pre_up[:slots])
+    for copy in copies[:n]:
+        copy.wait()
+    pre_gate = nt_dot(both, gate[...])
+    for copy in copies[n:]:
+        copy.wait()
+    pre_up = nt_dot(both, up[...])
+    act, _, _ = gate_terms(of_batch(pre_gate, 0, sources), of_batch(pre_up, 0, sources))
     act_ref[...] = act
-    inner, to_gate, to_up = gate_terms(pre_gate[slots:], pre_up[slots:])
+    inner, to_gate, to_up = gate_terms(
+        of_batch(pre_gate, 1, sources), of_batch(pre_up, 1, sources)
+    )
     inner_ref[...] = inner
     to_gate_ref[...] = to_gate
     to_up_ref[...] = to_up
 
 
 def far_kernel(n, *refs):
-    got_hbm, pieces, refs = refs[0], refs[1 : 1 + 3 * n], refs[1 + 3 * n :]
+    got, pieces, refs = refs[0], refs[1 : 1 + 3 * n], refs[1 + 3 * n :]
     sum_f, sum_b, change_ref, act, inner, to_gate, to_up, out_hbm = refs[:8]
-    upstream, gate, up, down, out, sems = refs[8:]
+    gate, up, down, out, sems = refs[8:]
     width = gate.shape[1]
     pairs = load_pieces(pieces[2 * n :], down, n)
-    pairs += [(got_hbm.at[:, pl.ds(2 * width, width)], upstream)]
     pairs += load_pieces(pieces[:n], gate, n)
     pairs += load_pieces(pieces[n : 2 * n], up, n)
     copies = start_copies(pairs, sems)
@@ -303,9 +322,9 @@
         copy.start()
         stores.append(copy)
 
-    for copy in copies[: n + 1]:
-        copy.wait()
-    pulled = nt_dot(upstream[...], down[...])
+    for copy in copies[:n]:
+        copy.wait()
+    pulled = nt_dot(gradient_rows(got), down[...])
     change = jnp.sum(inner[...].astype(F32) * pulled, axis=1, keepdims=True)
     out[:, 2 * width :] = (change_ref[...] + change).astype(BF16)
     grad_gate = (pulled * to_gate[...]).astype(BF16)
@@ -316,7 +335,7 @@
             + jnp.dot(act[...], down[:, at : at + STEP], preferred_element_type=F32)
         ).astype(BF16)
     store(0, width)
-    for copy in copies[n + 1 :]:
+    for copy in copies[n:]:
         copy.wait()
     for at in range(0, width, STEP):
         out[:, width + at : width + at + STEP] = (
@@ -330,7 +349,7 @@
 
 
 def expert_calls(got, near_pieces, far_pieces, after_near):
-    slots = got.shape[0]
+    slots = got.shape[0] * got.shape[1] // 3
     n = 2
     quarter, width = near_pieces[0].shape
     hidden = n * quarter
@@ -354,10 +373,10 @@
     sums = pl.pallas_call(
         functools.partial(near_kernel, n),
         out_shape=[shape(width, F32), shape(width, F32), shape(128, F32)],
-        in_specs=[anywhere] + [HBM_SPEC] * 6,
+        in_specs=[vmem] + [HBM_SPEC] * 6,
         out_specs=[vmem] * 3,
-        scratch_shapes=[pltpu.VMEM((3 * slots, width), BF16), full, full, full]
-        + [pltpu.SemaphoreType.DMA((9,))],
+        scratch_shapes=[full, full, full]
+        + [pltpu.SemaphoreType.DMA((6,))],
         name="near_share",
         **params(8, 32),
     )(got, *near_pieces)
@@ -370,21 +389,21 @@
             shape(hidden, F32),
             shape(hidden, F32),
         ],
-        in_specs=[anywhere] + [HBM_SPEC, anywhere] * 2,
+        in_specs=[vmem] + [HBM_SPEC, anywhere] * 2,
         out_specs=[vmem] * 4,
-        scratch_shapes=[pltpu.VMEM((2 * slots, width), BF16), full, full]
-        + [pltpu.SemaphoreType.DMA((6,))],
+        scratch_shapes=[full, full]
+        + [pltpu.SemaphoreType.DMA((4,))],
         name="far_front",
         **params(4, 24),
     )(got, *far_pieces[:4])
     return pl.pallas_call(
         functools.partial(far_kernel, n),
         out_shape=pltpu.HBM((slots, 2 * width + 128), BF16),
-        in_specs=[anywhere] + [HBM_SPEC, anywhere] * 3 + [vmem] * 7,
+        in_specs=[vmem] + [HBM_SPEC, anywhere] * 3 + [vmem] * 7,
         out_specs=HBM_SPEC,
-        scratch_shapes=[pltpu.VMEM((slots, width), BF16), full, full, full]
+        scratch_shapes=[full, full, full]
         + [pltpu.VMEM((slots, 2 * width + 128), BF16)]
-        + [pltpu.SemaphoreType.DMA((9,))],
+        + [pltpu.SemaphoreType.DMA((8,))],
         name="far_rest",
         **params(4, 32),
     )(got, *far_pieces, *sums, *fronts)
@@ -450,14 +469,10 @@
     )(*args)
 
 
-def trade(rows):
-    groups = trade_groups()
-    count = len(groups[0])
-    blocks = rows.reshape(count, rows.shape[0] // count, rows.shape[1])
-    blocks = lax.all_to_all(
-        blocks, "expert", 0, 0, axis_index_groups=groups, tiled=True
-    )
-    return blocks.reshape(rows.shape)
+def trade(blocks):
+    return lax.all_to_all(
+        blocks, "expert", 0, 0, axis_index_groups=trade_groups(), tiled=True
+    )
 
 
 def paired(held, passed):
@@ -498,7 +513,7 @@
         return paired(pieces, crossed), sums
 
     out = expert_calls(got, paired(own, near), far, cross)
-    back = trade(out)
+    back = trade(out.reshape(send.shape[0], -1, out.shape[1])).reshape(out.shape)
     mixed, input_grad = end_call(
         back, fsel, fcol, bsel, bcol, section_input[0], saved_input[0], grad_input[0], norm_gain, router_t
     )

time: 220 us -> 220 us (level)
  no operation moved by 1% of the time
where the time goes in v3:
time: 220 us
  waiting for transfers between devices  77.8 us (35%)
  blocking collectives  65.3 us (30%)
  starting transfers between devices  51.8 us (24%)
  Pallas kernels  21.4 us (10%)
  local copies, waits for them, and re-layouts  2.44 us (1%)
    all_to_all x1, blocking collectives, trade(): lax.all_to_all(blocks, 'expert', 0, 0, axis_index_groups=trade_groups(),...  65.3 us
    ppermute x3, waiting for transfers between devices, on_device(): far = [lax.ppermute(w, 'expert', across) for w in own]  64.4 us
    all_to_all x1, starting transfers between devices, trade(): lax.all_to_all(blocks, 'expert', 0, 0, axis_index_groups=trade_groups(),...  15.8 us
    ppermute x2, waiting for transfers between devices, shifted(): lax.ppermute(block, 'section', [((i - distance) % n, i) for i in range(n)])  10.7 us
    ppermute x3, starting transfers between devices, cross(): crossed = [lax.ppermute(w, 'expert', between) for w in pieces]  10.6 us
    ppermute x3, starting transfers between devices, on_device(): far = [lax.ppermute(w, 'expert', across) for w in own]  10.1 us
    ppermute x3, starting transfers between devices, on_device(): near = [lax.ppermute(w, 'expert', between) for w in own]  8.35 us
    ppermute x2, starting transfers between devices, shifted(): lax.ppermute(block, 'section', [((i - distance) % n, i) for i in range(n)])  6.99 us
  transfers between devices with their start and end apart: 12, of which 6 were waited for; matrix products, arithmetic and copies ran while one was open for 0% of the time, Pallas kernels for 7%

profile of v3, /device:TPU:1, one launch (start us, length us, event | category | flops | bytes accessed | tf_op | source)
XLA Modules:
  0.0 219.6 jit_solution(11350069058366758576)
XLA Ops:
  0.6 4.8 %collective-permute-start = (bf16[192,2048]{1,0:T(8,128)(2,1)}, bf16[192,2048]{1,0:T(8,128)(2,1)}, u32[]{:S(2)}, u32[]{:S(2)}) collective-permute-start(bf16[192,2048]{1,0:T(8,128)(2,1)} %bitcast.37), channel_id=1, source_target_pairs={{0,2},{1,3},{2,0},{3,1},{4,6},{5,7},{6,4},{7,5},{8,10},{9,11},{10,... | collective-permute-start | bytes 2359304 | tf_op jit(solution)/shard_map/ppermute | solution.py:496
  5.5 4.0 %prologue.1 = (bf16[16,48,2048]{2,1,0:T(8,128)(2,1)}, bf16[2,256,96]{2,1,0:T(8,128)(2,1)S(1)}, f32[96,128]{1,0:T(8,128)S(1)}, bf16[2,256,96]{2,1,0:T(8,128)(2,1)S(1)}, f32[96,128]{1,0:T(8,128)S(1)}) custom-call(bf16[96,2048]{1,0:T(8,128)(2,1)} %bitcast.24, bf16[96,2048]{1,0:T(8,128)(2,1)} %bitcast.26, bf16[96,2048]{1,0:T(8,128)(2,1)} %bitcast.28, ...), custom_call_target="tpu_custom_call" | custom-call | flops 301989888 | bytes 5242880 | tf_op jit(solution)/shard_map/prologue/pallas_call | solution.py:193
  9.5 9.4 %collective-permute-done.refs_1_ = bf16[192,2048]{1,0:T(8,128)(2,1)} collective-permute-done((bf16[192,2048]{1,0:T(8,128)(2,1)}, bf16[192,2048]{1,0:T(8,128)(2,1)}, u32[]{:S(2)}, u32[]{:S(2)}) %collective-permute-start) | collective-permute-done | bytes 786464 | tf_op jit(solution)/shard_map/ppermute | solution.py:496
  18.9 15.8 %all-to-all-start = ((bf16[16,48,2048]{2,1,0:T(8,128)(2,1)}), bf16[16,48,2048]{2,1,0:T(8,128)(2,1)S(1)}, u32[]{:S(2)}, u32[]{:S(2)}) async-start(bf16[16,48,2048]{2,1,0:T(8,128)(2,1)} %get-tuple-element.23), calls=%async_computation | async-start | bytes 6291456 | tf_op jit(solution)/shard_map/all_to_all | solution.py:473
  34.7 3.7 %collective-permute-start.5 = (bf16[192,2048]{1,0:T(8,128)(2,1)}, bf16[192,2048]{1,0:T(8,128)(2,1)S(1)}, u32[]{:S(2)}, u32[]{:S(2)}) collective-permute-start(bf16[192,2048]{1,0:T(8,128)(2,1)} %bitcast.38), channel_id=1, source_target_pairs={{0,1},{1,0},{2,3},{3,2},{4,5},{5,4},{6,7},{7,6},{8,9},{9,8},{10,11... | collective-permute-start | bytes 2359304 | tf_op jit(solution)/shard_map/ppermute | solution.py:497
  38.4 1.9 collective-permute-start.6
  40.4 3.1 %collective-permute-start.2 = (bf16[192,2048]{1,0:T(8,128)(2,1)}, bf16[192,2048]{1,0:T(8,128)(2,1)}, u32[]{:S(2)}, u32[]{:S(2)}) collective-permute-start(bf16[192,2048]{1,0:T(8,128)(2,1)} %bitcast.41), channel_id=1, source_target_pairs={{0,2},{1,3},{2,0},{3,1},{4,6},{5,7},{6,4},{7,5},{8,10},{9,11},{10,... | collective-permute-start | bytes 2359304 | tf_op jit(solution)/shard_map/ppermute | solution.py:496
  43.5 2.7 %collective-permute-start.7 = (bf16[192,2048]{1,0:T(8,128)(2,1)}, bf16[192,2048]{1,0:T(8,128)(2,1)}, u32[]{:S(2)}, u32[]{:S(2)}) collective-permute-start(bf16[192,2048]{1,0:T(8,128)(2,1)} %bitcast.43), channel_id=1, source_target_pairs={{0,1},{1,0},{2,3},{3,2},{4,5},{5,4},{6,7},{7,6},{8,9},{9,8},{10,11... | collective-permute-start | bytes 2359304 | tf_op jit(solution)/shard_map/ppermute | solution.py:497
  46.2 2.2 %collective-permute-start.4 = (bf16[192,2048]{1,0:T(8,128)(2,1)}, bf16[192,2048]{1,0:T(8,128)(2,1)}, u32[]{:S(2)}, u32[]{:S(2)}) collective-permute-start(bf16[192,2048]{1,0:T(8,128)(2,1)} %bitcast.44), channel_id=1, source_target_pairs={{0,2},{1,3},{2,0},{3,1},{4,6},{5,7},{6,4},{7,5},{8,10},{9,11},{10,... | collective-permute-start | bytes 2359304 | tf_op jit(solution)/shard_map/ppermute | solution.py:496
  48.4 0.0 collective-permute-done.5.refs_2_
  48.4 0.0 copy-start.5
  48.4 2.2 %collective-permute-start.1 = (bf16[192,2048]{1,0:T(8,128)(2,1)}, bf16[192,2048]{1,0:T(8,128)(2,1)}, u32[]{:S(2)}, u32[]{:S(2)}) collective-permute-start(bf16[192,2048]{1,0:T(8,128)(2,1)} %collective-permute-done.refs_1_), channel_id=1, source_target_pairs={{0,1},{1,0},{2,3},{3,2},{4,5},{5,4},{6,7},{7,6},{8,9},{9,8},{10,11... | collective-permute-start | bytes 2359304 | tf_op jit(solution)/shard_map/ppermute | solution.py:512
  50.6 53.0 %collective-permute-done.2.refs_3_ = bf16[192,2048]{1,0:T(8,128)(2,1)} collective-permute-done((bf16[192,2048]{1,0:T(8,128)(2,1)}, bf16[192,2048]{1,0:T(8,128)(2,1)}, u32[]{:S(2)}, u32[]{:S(2)}) %collective-permute-start.2) | collective-permute-done | bytes 786464 | tf_op jit(solution)/shard_map/ppermute | solution.py:496
  103.6 4.8 %collective-permute-start.3 = (bf16[192,2048]{1,0:T(8,128)(2,1)}, bf16[192,2048]{1,0:T(8,128)(2,1)}, u32[]{:S(2)}, u32[]{:S(2)}) collective-permute-start(bf16[192,2048]{1,0:T(8,128)(2,1)} %collective-permute-done.2.refs_3_), channel_id=1, source_target_pairs={{0,1},{1,0},{2,3},{3,2},{4,5},{5,4},{6,7},{7,6},{8,9},{9,8},{10,11... | collective-permute-start | bytes 2359304 | tf_op jit(solution)/shard_map/ppermute | solution.py:512
  108.4 0.0 collective-permute-done.6.refs_4_
  108.4 0.0 copy-done.5
  108.4 0.0 copy-start.6
  108.4 0.9 copy-done.6
  109.3 0.0 collective-permute-done.7.refs_6_
  109.4 2.6 %all-to-all-done.refs_0_ = bf16[16,48,2048]{2,1,0:T(8,128)(2,1)S(1)} async-done(((bf16[16,48,2048]{2,1,0:T(8,128)(2,1)}), bf16[16,48,2048]{2,1,0:T(8,128)(2,1)S(1)}, u32[]{:S(2)}, u32[]{:S(2)}) %all-to-all-start) | async-done | bytes 3145760 | tf_op jit(solution)/shard_map/all_to_all | solution.py:473
  112.0 6.4 %near_share.1 = (f32[256,2048]{1,0:T(8,128)S(1)}, f32[256,2048]{1,0:T(8,128)S(1)}, f32[256,128]{1,0:T(8,128)S(1)}) custom-call(bf16[16,48,2048]{2,1,0:T(8,128)(2,1)S(1)} %all-to-all-done.refs_0_, bf16[192,2048]{1,0:T(8,128)(2,1)} %bitcast.39, bf16[192,2048]{1,0:T(8,128)(2,1)} %copy-done.5, bf16[192,2048]{1,0:T(8,128)(2,1)} %bitcast.42, ...), custom_call_target="tpu_custom_call" | custom-call | flops 3221225472 | bytes 8388608 | tf_op jit(solution)/shard_map/near_share/pallas_call | solution.py:373
  118.4 2.0 collective-permute-done.4.refs_5_
  120.4 3.6 %collective-permute-start.8 = (bf16[192,2048]{1,0:T(8,128)(2,1)}, bf16[192,2048]{1,0:T(8,128)(2,1)S(1)}, u32[]{:S(2)}, u32[]{:S(2)}) collective-permute-start(bf16[192,2048]{1,0:T(8,128)(2,1)} %collective-permute-done.4.refs_5_), channel_id=1, source_target_pairs={{0,1},{1,0},{2,3},{3,2},{4,5},{5,4},{6,7},{7,6},{8,9},{9,8},{10,11... | collective-permute-start | bytes 2359304 | tf_op jit(solution)/shard_map/ppermute | solution.py:512
  124.0 0.0 collective-permute-done.3.refs_4_
  124.0 0.0 collective-permute-done.1.refs_2_
  124.0 4.0 %far_front.1 = (bf16[256,384]{1,0:T(8,128)(2,1)S(1)}, bf16[256,384]{1,0:T(8,128)(2,1)S(1)}, f32[256,384]{1,0:T(8,128)S(1)}, f32[256,384]{1,0:T(8,128)S(1)}) custom-call(bf16[16,48,2048]{2,1,0:T(8,128)(2,1)S(1)} %all-to-all-done.refs_0_, bf16[192,2048]{1,0:T(8,128)(2,1)} %collective-permute-done.refs_1_, bf16[192,2048]{1,0:T(8,128)(2,1)} %collective-permute-done.1.refs_2_, ...), custom_call_target="tpu_custom_call" | custom-call | flops 1610612736 | bytes 8388608 | tf_op jit(solution)/shard_map/far_front/pallas_call | solution.py:384
  128.0 0.0 collective-permute-done.8.refs_6_
  128.0 4.8 %far_rest.1 = bf16[256,4224]{1,0:T(8,128)(2,1)} custom-call(bf16[16,48,2048]{2,1,0:T(8,128)(2,1)S(1)} %all-to-all-done.refs_0_, bf16[192,2048]{1,0:T(8,128)(2,1)} %collective-permute-done.refs_1_, bf16[192,2048]{1,0:T(8,128)(2,1)} %collective-permute-done.1.refs_2_, bf16[192,2048]{1,0:T(8,128)(2,1)} %collective-permute-done.2.refs_3_, ...), custom_call_target="tpu_custom_call" | custom-call | flops 1610612736 | bytes 8388608 | tf_op jit(solution)/shard_map/far_rest/pallas_call | solution.py:399
  132.8 0.0 copy-start
  132.8 0.0 copy-start.1
  132.9 0.0 copy-start.2
  132.9 0.0 copy-start.3
  132.9 0.0 copy-start.4
  132.9 65.3 %all_to_all.10 = bf16[16,16,4224]{2,1,0:T(8,128)(2,1)S(1)} all-to-all(bf16[16,16,4224]{2,1,0:T(8,128)(2,1)} %bitcast.34), channel_id=1, replica_groups={{0,4,10,14,16,20,26,30,32,36,42,46,48,52,58,62},{1,5,11,15,17,21,27,31,..., dimensions={0} | all-to-all | bytes 4325376 | tf_op jit(solution)/shard_map/all_to_all | solution.py:473
  198.2 0.0 copy-done
  198.2 0.0 copy-done.1
  198.2 0.0 copy-done.2
  198.2 0.0 copy-done.3
  198.2 0.0 copy-done.4
  198.2 2.1 finish.1
  200.3 5.1 %collective-permute-start.10 = (bf16[1,96,2048]{2,1,0:T(8,128)(2,1)S(1)}, bf16[1,96,2048]{2,1,0:T(8,128)(2,1)S(1)}, u32[]{:S(2)}, u32[]{:S(2)}) collective-permute-start(bf16[1,96,2048]{2,1,0:T(8,128)(2,1)S(1)} %bitcast.33), channel_id=1, source_target_pairs={{64,0},{128,64},{192,128},{256,192},{320,256},{384,320},{448,384},... | collective-permute-start | bytes 1179656 | tf_op jit(solution)/shard_map/ppermute | solution.py:44
  205.4 1.9 collective-permute-start.9
  207.3 5.7 %collective-permute-done.10 = bf16[1,96,2048]{2,1,0:T(8,128)(2,1)S(1)} collective-permute-done((bf16[1,96,2048]{2,1,0:T(8,128)(2,1)S(1)}, bf16[1,96,2048]{2,1,0:T(8,128)(2,1)S(1)}, u32[]{:S(2)}, u32[]{:S(2)}) %collective-permute-start.10) | collective-permute-done | bytes 393248 | tf_op jit(solution)/shard_map/ppermute | solution.py:44
  213.1 5.0 %collective-permute-done.9 = bf16[1,96,2048]{2,1,0:T(8,128)(2,1)S(1)} collective-permute-done((bf16[1,96,2048]{2,1,0:T(8,128)(2,1)S(1)}, bf16[1,96,2048]{2,1,0:T(8,128)(2,1)S(1)}, u32[]{:S(2)}, u32[]{:S(2)}) %collective-permute-start.9) | collective-permute-done | bytes 393248 | tf_op jit(solution)/shard_map/ppermute | solution.py:44
  218.1 0.7 copy.14
  218.8 0.7 copy.15
Async XLA Ops:
  0.6 18.3 %collective-permute-start = (bf16[192,2048]{1,0:T(8,128)(2,1)}, bf16[192,2048]{1,0:T(8,128)(2,1)}, u32[]{:S(2)}, u32[]{:S(2)}) collective-permute-start(bf16[192,2048]{1,0:T(8,128)(2,1)} %bitcast.37), channel_id=1, source_target_pairs={{0,2},{1,3},{2,0},{3,1},{4,6},{5,7},{6,4},{7,5},{8,10},{9,11},{10,... | collective-permute-start | bytes 2359304 | tf_op jit(solution)/shard_map/ppermute | solution.py:496
  18.9 93.1 %all-to-all-start = ((bf16[16,48,2048]{2,1,0:T(8,128)(2,1)}), bf16[16,48,2048]{2,1,0:T(8,128)(2,1)S(1)}, u32[]{:S(2)}, u32[]{:S(2)}) async-start(bf16[16,48,2048]{2,1,0:T(8,128)(2,1)} %get-tuple-element.23), calls=%async_computation | async-start | bytes 6291456 | tf_op jit(solution)/shard_map/all_to_all | solution.py:473
  34.7 13.7 %collective-permute-start.5 = (bf16[192,2048]{1,0:T(8,128)(2,1)}, bf16[192,2048]{1,0:T(8,128)(2,1)S(1)}, u32[]{:S(2)}, u32[]{:S(2)}) collective-permute-start(bf16[192,2048]{1,0:T(8,128)(2,1)} %bitcast.38), channel_id=1, source_target_pairs={{0,1},{1,0},{2,3},{3,2},{4,5},{5,4},{6,7},{7,6},{8,9},{9,8},{10,11... | collective-permute-start | bytes 2359304 | tf_op jit(solution)/shard_map/ppermute | solution.py:497
  38.4 70.0 %collective-permute-start.6 = (bf16[192,2048]{1,0:T(8,128)(2,1)}, bf16[192,2048]{1,0:T(8,128)(2,1)S(1)}, u32[]{:S(2)}, u32[]{:S(2)}) collective-permute-start(bf16[192,2048]{1,0:T(8,128)(2,1)} %bitcast.40), channel_id=1, source_target_pairs={{0,1},{1,0},{2,3},{3,2},{4,5},{5,4},{6,7},{7,6},{8,9},{9,8},{10,11... | collective-permute-start | bytes 2359304 | tf_op jit(solution)/shard_map/ppermute | solution.py:497
  40.4 63.2 %collective-permute-start.2 = (bf16[192,2048]{1,0:T(8,128)(2,1)}, bf16[192,2048]{1,0:T(8,128)(2,1)}, u32[]{:S(2)}, u32[]{:S(2)}) collective-permute-start(bf16[192,2048]{1,0:T(8,128)(2,1)} %bitcast.41), channel_id=1, source_target_pairs={{0,2},{1,3},{2,0},{3,1},{4,6},{5,7},{6,4},{7,5},{8,10},{9,11},{10,... | collective-permute-start | bytes 2359304 | tf_op jit(solution)/shard_map/ppermute | solution.py:496
  43.5 65.9 %collective-permute-start.7 = (bf16[192,2048]{1,0:T(8,128)(2,1)}, bf16[192,2048]{1,0:T(8,128)(2,1)}, u32[]{:S(2)}, u32[]{:S(2)}) collective-permute-start(bf16[192,2048]{1,0:T(8,128)(2,1)} %bitcast.43), channel_id=1, source_target_pairs={{0,1},{1,0},{2,3},{3,2},{4,5},{5,4},{6,7},{7,6},{8,9},{9,8},{10,11... | collective-permute-start | bytes 2359304 | tf_op jit(solution)/shard_map/ppermute | solution.py:497
  46.2 74.3 %collective-permute-start.4 = (bf16[192,2048]{1,0:T(8,128)(2,1)}, bf16[192,2048]{1,0:T(8,128)(2,1)}, u32[]{:S(2)}, u32[]{:S(2)}) collective-permute-start(bf16[192,2048]{1,0:T(8,128)(2,1)} %bitcast.44), channel_id=1, source_target_pairs={{0,2},{1,3},{2,0},{3,1},{4,6},{5,7},{6,4},{7,5},{8,10},{9,11},{10,... | collective-permute-start | bytes 2359304 | tf_op jit(solution)/shard_map/ppermute | solution.py:496
  48.4 60.0 %copy-start.5 = (bf16[192,2048]{1,0:T(8,128)(2,1)}, bf16[192,2048]{1,0:T(8,128)(2,1)S(1)}, u32[]{:S(2)}) copy-start(bf16[192,2048]{1,0:T(8,128)(2,1)S(1)} %collective-permute-done.5.refs_2_) | copy-start | bytes 2359300
  48.4 75.6 %collective-permute-start.1 = (bf16[192,2048]{1,0:T(8,128)(2,1)}, bf16[192,2048]{1,0:T(8,128)(2,1)}, u32[]{:S(2)}, u32[]{:S(2)}) collective-permute-start(bf16[192,2048]{1,0:T(8,128)(2,1)} %collective-permute-done.refs_1_), channel_id=1, source_target_pairs={{0,1},{1,0},{2,3},{3,2},{4,5},{5,4},{6,7},{7,6},{8,9},{9,8},{10,11... | collective-permute-start | bytes 2359304 | tf_op jit(solution)/shard_map/ppermute | solution.py:512
  103.6 20.4 %collective-permute-start.3 = (bf16[192,2048]{1,0:T(8,128)(2,1)}, bf16[192,2048]{1,0:T(8,128)(2,1)}, u32[]{:S(2)}, u32[]{:S(2)}) collective-permute-start(bf16[192,2048]{1,0:T(8,128)(2,1)} %collective-permute-done.2.refs_3_), channel_id=1, source_target_pairs={{0,1},{1,0},{2,3},{3,2},{4,5},{5,4},{6,7},{7,6},{8,9},{9,8},{10,11... | collective-permute-start | bytes 2359304 | tf_op jit(solution)/shard_map/ppermute | solution.py:512
  108.4 0.9 copy-start.6
  120.4 7.6 %collective-permute-start.8 = (bf16[192,2048]{1,0:T(8,128)(2,1)}, bf16[192,2048]{1,0:T(8,128)(2,1)S(1)}, u32[]{:S(2)}, u32[]{:S(2)}) collective-permute-start(bf16[192,2048]{1,0:T(8,128)(2,1)} %collective-permute-done.4.refs_5_), channel_id=1, source_target_pairs={{0,1},{1,0},{2,3},{3,2},{4,5},{5,4},{6,7},{7,6},{8,9},{9,8},{10,11... | collective-permute-start | bytes 2359304 | tf_op jit(solution)/shard_map/ppermute | solution.py:512
  132.8 65.3 %copy-start = (bf16[1,96,2048]{2,1,0:T(8,128)(2,1)S(1)}, bf16[1,96,2048]{2,1,0:T(8,128)(2,1)}, u32[]{:S(2)}) copy-start(bf16[1,96,2048]{2,1,0:T(8,128)(2,1)} %param.10) | copy-start | bytes 1179652
  132.8 65.3 %copy-start.1 = (bf16[1,96,2048]{2,1,0:T(8,128)(2,1)S(1)}, bf16[1,96,2048]{2,1,0:T(8,128)(2,1)}, u32[]{:S(2)}) copy-start(bf16[1,96,2048]{2,1,0:T(8,128)(2,1)} %param.11) | copy-start | bytes 1179652
  132.9 65.3 %copy-start.2 = (bf16[1,96,2048]{2,1,0:T(8,128)(2,1)S(1)}, bf16[1,96,2048]{2,1,0:T(8,128)(2,1)}, u32[]{:S(2)}) copy-start(bf16[1,96,2048]{2,1,0:T(8,128)(2,1)} %param.12) | copy-start | bytes 1179652
  132.9 65.3 %copy-start.3 = (bf16[1,2048,16]{1,2,0:T(8,128)(2,1)S(1)}, bf16[1,2048,16]{1,2,0:T(8,128)(2,1)}, u32[]{:S(2)}) copy-start(bf16[1,2048,16]{1,2,0:T(8,128)(2,1)} %param.16) | copy-start | bytes 196612
  132.9 65.3 %copy-start.4 = (f32[1,2048]{1,0:T(1,128)S(1)}, f32[1,2048]{1,0:T(1,128)}, u32[]{:S(2)}) copy-start(f32[1,2048]{1,0:T(1,128)} %gain_ref.1) | copy-start | bytes 24580
  200.3 12.7 %collective-permute-start.10 = (bf16[1,96,2048]{2,1,0:T(8,128)(2,1)S(1)}, bf16[1,96,2048]{2,1,0:T(8,128)(2,1)S(1)}, u32[]{:S(2)}, u32[]{:S(2)}) collective-permute-start(bf16[1,96,2048]{2,1,0:T(8,128)(2,1)S(1)} %bitcast.33), channel_id=1, source_target_pairs={{64,0},{128,64},{192,128},{256,192},{320,256},{384,320},{448,384},... | collective-permute-start | bytes 1179656 | tf_op jit(solution)/shard_map/ppermute | solution.py:44
  205.4 12.7 %collective-permute-start.9 = (bf16[1,96,2048]{2,1,0:T(8,128)(2,1)S(1)}, bf16[1,96,2048]{2,1,0:T(8,128)(2,1)S(1)}, u32[]{:S(2)}, u32[]{:S(2)}) collective-permute-start(bf16[1,96,2048]{2,1,0:T(8,128)(2,1)S(1)} %bitcast.32), channel_id=1, source_target_pairs={{448,0},{0,64},{64,128},{128,192},{192,256},{256,320},{320,384},{3... | collective-permute-start | bytes 1179656 | tf_op jit(solution)/shard_map/ppermute | solution.py:44
